TPU v7x, 32 devices: a whole 2x2x4 slice. The times are simulated.
32 devices in a mesh: dp: 8 (over y, x, core), ctx: 4 (over z).
Axes of the slice: x: 2, y: 2, z: 4, core: 2. Of those that a mesh axis runs over, the one named last changes fastest.
Arguments:
- tokens: bfloat16 [16, 1536, 960], P('dp', 'ctx'), may hold values from -6 to 6
- lengths: int32 [16, 3], P('dp'), may hold values from 1 to 1534, as said below
- gain_attn: bfloat16 [960], P('dp'), may hold values from 0.5 to 1.5
- w_query: bfloat16 [960, 960], P('dp'), may hold values from -0.1875 to 0.1875
- w_key: bfloat16 [960, 320], P('dp'), may hold values from -0.1875 to 0.1875
- w_value: bfloat16 [960, 320], P('dp'), may hold values from -0.1875 to 0.1875
- w_out: bfloat16 [960, 960], P(None, 'dp'), may hold values from -3.5 to 3.5
- gain_ffn: bfloat16 [960], P('dp'), may hold values from 0.5 to 1.5
- w_gate: bfloat16 [960, 2560], P('dp'), may hold values from -0.1875 to 0.1875
- w_up: bfloat16 [960, 2560], P('dp'), may hold values from -0.1875 to 0.1875
- w_down: bfloat16 [2560, 960], P(None, 'dp'), may hold values from -0.125 to 0.125
- cotangent: bfloat16 [16, 1536, 960], P('dp', 'ctx'), may hold values from -6 to 6
Outputs:
- output: bfloat16 [16, 1536, 960], P('dp', 'ctx')
- d_tokens: bfloat16 [16, 1536, 960], P('dp', 'ctx')
- grad_gain_attn: float32 [960], P('dp')
- grad_w_query: float32 [960, 960], P('dp')
- grad_w_key: float32 [960, 320], P('dp')
- grad_w_value: float32 [960, 320], P('dp')
- grad_w_out: float32 [960, 960], P(None, 'dp')
- grad_gain_ffn: float32 [960], P('dp')
- grad_w_gate: float32 [960, 2560], P('dp')
- grad_w_up: float32 [960, 2560], P('dp')
- grad_w_down: float32 [2560, 960], P(None, 'dp')
Inputs may be any that keep to these rules, and one draw needn't show every extreme that they name: Each row holds three document lengths summing to 1536; the first and the last are at most 96; in one row the first and the last are 1.
All inputs are finite; a program needn't handle non-finite values.
Results may differ from a plain program's by a relative error of at most 0.02.
Values may be sent and summed in bfloat16 or wider, within the bound.
A program may use at most 256 MiB of HBM per device.

v0:
```python
import math

import jax
import jax.numpy as jnp
from jax import lax
from jax.sharding import PartitionSpec as P

D = 960
H = 15
KVH = 5
HD = 64
FF = 2560


NORM_EPSILON = 1e-05
ROPE_BASE = 10000.0
MASKED_SCORE = -1e30


def norm_apply(values, gain_vec):
    return (
        values * lax.rsqrt(jnp.mean(values * values, -1, keepdims=True) + NORM_EPSILON) * gain_vec
    )


def rotate(values, positions):
    half_width = values.shape[-1] // 2
    frequency = ROPE_BASE ** (-jnp.arange(half_width, dtype=jnp.float32) / half_width)
    angles = positions.astype(jnp.float32)[:, None] * frequency[None, :]
    cosine = jnp.cos(angles)[:, None, :]
    sine_vals = jnp.sin(angles)[:, None, :]
    first_half = values[..., :half_width]
    second_half = values[..., half_width:]
    return jnp.concatenate(
        [
            first_half * cosine - second_half * sine_vals,
            second_half * cosine + first_half * sine_vals,
        ],
        -1,
    )


def doc_layout(doc_lengths, places):
    first_end = doc_lengths[0]
    second_end = doc_lengths[0] + doc_lengths[1]
    after_first = (places >= first_end).astype(jnp.int32)
    after_second = (places >= second_end).astype(jnp.int32)
    return (
        after_first + after_second,
        places - after_first * first_end - after_second * doc_lengths[1],
    )


def block_scores(queries, key_block, query_doc, query_pos, key_doc, key_pos, score_scale):
    scores = (
        jnp.einsum("nkgd,ckd->kgnc", queries, key_block, preferred_element_type=jnp.float32)
        * score_scale
    )
    allowed = (key_doc[None, :] == query_doc[:, None]) & (key_pos[None, :] <= query_pos[:, None])
    return (scores, allowed)


def gated(gate_in, up_in):
    return jax.nn.silu(gate_in) * up_in


def local(
    tokens,
    lengths,
    gain_attn,
    w_query,
    w_key,
    w_value,
    w_out,
    gain_ffn,
    w_gate,
    w_up,
    w_down,
    cotangent,
):
    tok_rows = tokens.shape[1]
    ctx_count = lax.axis_size("ctx")
    own_index = lax.axis_index("ctx")
    offset = own_index * tok_rows
    score_scale = 1.0 / math.sqrt(HD)
    groups = H // KVH
    query_places = offset + jnp.arange(tok_rows, dtype=jnp.int32)

    def micro_step(totals, packed):
        pack_tokens, doc_lengths, pack_cot = packed
        forward_set = (
            lax.all_gather(gain_attn, "dp", axis=0, tiled=True),
            lax.all_gather(w_query, "dp", axis=0, tiled=True),
            lax.all_gather(w_key, "dp", axis=0, tiled=True),
            lax.all_gather(w_value, "dp", axis=0, tiled=True),
            lax.all_gather(w_out, "dp", axis=1, tiled=True),
            lax.all_gather(gain_ffn, "dp", axis=0, tiled=True),
            lax.all_gather(w_gate, "dp", axis=0, tiled=True),
            lax.all_gather(w_up, "dp", axis=0, tiled=True),
            lax.all_gather(w_down, "dp", axis=1, tiled=True),
        )
        (
            gain_one,
            full_query,
            full_key,
            full_value,
            full_out,
            gain_two,
            full_gate,
            full_up,
            full_down,
        ) = forward_set
        query_doc, query_pos = doc_layout(doc_lengths, query_places)
        stream = pack_tokens.astype(jnp.float32)
        normed = norm_apply(stream, gain_one.astype(jnp.float32)).astype(jnp.bfloat16)
        query_lin = jnp.dot(normed, full_query, preferred_element_type=jnp.float32).reshape(
            tok_rows, H, HD
        )
        key_lin = jnp.dot(normed, full_key, preferred_element_type=jnp.float32).reshape(
            tok_rows, KVH, HD
        )
        value_lin = jnp.dot(normed, full_value, preferred_element_type=jnp.float32)
        queries = (
            rotate(query_lin, query_pos).astype(jnp.bfloat16).reshape(tok_rows, KVH, groups, HD)
        )
        keys_own = rotate(key_lin, query_pos).astype(jnp.bfloat16).reshape(tok_rows, KVH * HD)
        values_own = value_lin.astype(jnp.bfloat16)
        keys_all, values_all = (
            lax.all_gather(keys_own, "ctx", axis=0, tiled=True),
            lax.all_gather(values_own, "ctx", axis=0, tiled=True),
        )
        key_blocks = keys_all.reshape(ctx_count, tok_rows, KVH, HD)
        value_blocks = values_all.reshape(ctx_count, tok_rows, KVH, HD)
        block_starts = jnp.arange(ctx_count, dtype=jnp.int32) * tok_rows
        live_flags = jnp.ones((ctx_count,), jnp.bool_)
        block_places = block_starts[:, None] + jnp.arange(tok_rows, dtype=jnp.int32)[None, :]
        doc_blocks, pos_blocks = doc_layout(doc_lengths, block_places)
        block_parts = (key_blocks, value_blocks, doc_blocks, pos_blocks, live_flags)

        def find_top(running, key_part):
            key_block, value_block, doc_block, pos_block, live = key_part

            def find_update(state):
                row_top, denominator = state
                scores, allowed = block_scores(
                    queries, key_block, query_doc, query_pos, doc_block, pos_block, score_scale
                )
                new_top = jnp.maximum(
                    row_top, jnp.max(jnp.where(allowed, scores, MASKED_SCORE), -1)
                )
                expos = jnp.where(allowed, jnp.exp(scores - new_top[..., None]), 0.0)
                return (new_top, denominator * jnp.exp(row_top - new_top) + jnp.sum(expos, -1))

            return (lax.cond(live, find_update, lambda state: state, running), None)

        start_top = jnp.full((KVH, groups, tok_rows), MASKED_SCORE, jnp.float32)
        start_sum = jnp.zeros((KVH, groups, tok_rows), jnp.float32)
        (row_top, denominator), _ = lax.scan(find_top, (start_top, start_sum), block_parts)

        def probs_of(key_block, doc_block, pos_block):
            scores, allowed = block_scores(
                queries, key_block, query_doc, query_pos, doc_block, pos_block, score_scale
            )
            return jnp.where(
                allowed, jnp.exp(scores - row_top[..., None]) / denominator[..., None], 0.0
            )

        def weigh_values(accum, key_part):
            key_block, value_block, doc_block, pos_block, live = key_part

            def weigh_update(total):
                prob_low = probs_of(key_block, doc_block, pos_block).astype(jnp.bfloat16)
                return total + jnp.einsum(
                    "kgnc,ckd->nkgd", prob_low, value_block, preferred_element_type=jnp.float32
                )

            return (lax.cond(live, weigh_update, lambda total: total, accum), None)

        attn, _ = lax.scan(
            weigh_values, jnp.zeros((tok_rows, KVH, groups, HD), jnp.float32), block_parts
        )
        attn_low = attn.reshape(tok_rows, H * HD).astype(jnp.bfloat16)
        middle = stream + jnp.dot(attn_low, full_out, preferred_element_type=jnp.float32)
        normed_two = norm_apply(middle, gain_two.astype(jnp.float32)).astype(jnp.bfloat16)
        gate_lin = jnp.dot(normed_two, full_gate, preferred_element_type=jnp.float32)
        up_lin = jnp.dot(normed_two, full_up, preferred_element_type=jnp.float32)
        hidden_f, gate_pull = jax.vjp(gated, gate_lin, up_lin)
        hidden = hidden_f.astype(jnp.bfloat16)
        result = (middle + jnp.dot(hidden, full_down, preferred_element_type=jnp.float32)).astype(
            jnp.bfloat16
        )
        backward_set = (
            lax.all_gather(gain_attn, "dp", axis=0, tiled=True),
            lax.all_gather(w_query, "dp", axis=0, tiled=True),
            lax.all_gather(w_key, "dp", axis=0, tiled=True),
            lax.all_gather(w_value, "dp", axis=0, tiled=True),
            lax.all_gather(w_out, "dp", axis=1, tiled=True),
            lax.all_gather(gain_ffn, "dp", axis=0, tiled=True),
            lax.all_gather(w_gate, "dp", axis=0, tiled=True),
            lax.all_gather(w_up, "dp", axis=0, tiled=True),
            lax.all_gather(w_down, "dp", axis=1, tiled=True),
        )
        (
            back_gain_one,
            back_query,
            back_key,
            back_value,
            back_out,
            back_gain_two,
            back_gate,
            back_up,
            back_down,
        ) = backward_set
        grad_out = pack_cot.astype(jnp.float32)
        d_down = jnp.einsum("nf,nd->fd", hidden, pack_cot, preferred_element_type=jnp.float32)
        d_hidden = jnp.einsum("nd,fd->nf", pack_cot, back_down, preferred_element_type=jnp.float32)
        d_gate, d_up = gate_pull(d_hidden)
        d_gate_low = d_gate.astype(jnp.bfloat16)
        d_up_low = d_up.astype(jnp.bfloat16)
        d_wgate = jnp.einsum(
            "nd,nf->df", normed_two, d_gate_low, preferred_element_type=jnp.float32
        )
        d_wup = jnp.einsum("nd,nf->df", normed_two, d_up_low, preferred_element_type=jnp.float32)
        d_normed_two = jnp.einsum(
            "nf,df->nd", d_gate_low, back_gate, preferred_element_type=jnp.float32
        ) + jnp.einsum("nf,df->nd", d_up_low, back_up, preferred_element_type=jnp.float32)
        _, norm_two_pull = jax.vjp(norm_apply, middle, back_gain_two.astype(jnp.float32))
        d_middle_norm, d_gain_two = norm_two_pull(d_normed_two)
        d_middle = grad_out + d_middle_norm
        d_mixed = d_middle.astype(jnp.bfloat16)
        d_wout = jnp.einsum("nq,nd->qd", attn_low, d_mixed, preferred_element_type=jnp.float32)
        d_attn = (
            jnp.einsum("nd,qd->nq", d_mixed, back_out, preferred_element_type=jnp.float32)
            .astype(jnp.bfloat16)
            .reshape(tok_rows, KVH, groups, HD)
        )

        def delta_block(accum, key_part):
            key_block, value_block, doc_block, pos_block, live = key_part

            def delta_update(total):
                probs = probs_of(key_block, doc_block, pos_block)
                d_probs = jnp.einsum(
                    "nkgd,ckd->kgnc", d_attn, value_block, preferred_element_type=jnp.float32
                )
                return total + jnp.sum(probs * d_probs, -1)

            return (lax.cond(live, delta_update, lambda total: total, accum), None)

        row_delta, _ = lax.scan(
            delta_block, jnp.zeros((KVH, groups, tok_rows), jnp.float32), block_parts
        )

        def block_grads(key_block, value_block, doc_block, pos_block):
            probs = probs_of(key_block, doc_block, pos_block)
            prob_low = probs.astype(jnp.bfloat16)
            d_probs = jnp.einsum(
                "nkgd,ckd->kgnc", d_attn, value_block, preferred_element_type=jnp.float32
            )
            d_scores = (probs * (d_probs - row_delta[..., None])).astype(jnp.bfloat16)
            query_part = (
                jnp.einsum(
                    "kgnc,ckd->nkgd", d_scores, key_block, preferred_element_type=jnp.float32
                )
                * score_scale
            )
            key_grad = (
                jnp.einsum("kgnc,nkgd->ckd", d_scores, queries, preferred_element_type=jnp.float32)
                * score_scale
            )
            value_grad = jnp.einsum(
                "kgnc,nkgd->ckd", prob_low, d_attn, preferred_element_type=jnp.float32
            )
            return (
                query_part,
                key_grad.reshape(tok_rows, KVH * HD),
                value_grad.reshape(tok_rows, KVH * HD),
            )

        def back_block(query_grad, key_part):
            key_block, value_block, doc_block, pos_block, live = key_part

            def work(unused):
                return block_grads(key_block, value_block, doc_block, pos_block)

            def skipped(unused):
                return (
                    jnp.zeros((tok_rows, KVH, groups, HD), jnp.float32),
                    jnp.zeros((tok_rows, KVH * HD), jnp.float32),
                    jnp.zeros((tok_rows, KVH * HD), jnp.float32),
                )

            query_part, key_grad, value_grad = lax.cond(live, work, skipped, query_grad)
            return (query_grad + query_part, (key_grad, value_grad))

        zero_query = jnp.zeros((tok_rows, KVH, groups, HD), jnp.float32)
        d_queries, (key_grads, value_grads) = lax.scan(back_block, zero_query, block_parts)
        key_terms = key_grads.reshape(ctx_count * tok_rows, KVH * HD)
        value_terms = value_grads.reshape(ctx_count * tok_rows, KVH * HD)
        d_keys, d_values = (
            lax.psum_scatter(
                key_terms.astype(jnp.bfloat16), "ctx", scatter_dimension=0, tiled=True
            ).astype(jnp.float32),
            lax.psum_scatter(
                value_terms.astype(jnp.bfloat16), "ctx", scatter_dimension=0, tiled=True
            ).astype(jnp.float32),
        )
        _, rope_query = jax.vjp(lambda rotated_in: rotate(rotated_in, query_pos), query_lin)
        _, rope_key = jax.vjp(lambda rotated_in: rotate(rotated_in, query_pos), key_lin)
        d_query_low = (
            rope_query(d_queries.reshape(tok_rows, H, HD))[0]
            .reshape(tok_rows, H * HD)
            .astype(jnp.bfloat16)
        )
        d_key_low = (
            rope_key(d_keys.reshape(tok_rows, KVH, HD))[0]
            .reshape(tok_rows, KVH * HD)
            .astype(jnp.bfloat16)
        )
        d_value_low = d_values.astype(jnp.bfloat16)
        d_wquery = jnp.einsum("nd,nq->dq", normed, d_query_low, preferred_element_type=jnp.float32)
        d_wkey = jnp.einsum("nd,nq->dq", normed, d_key_low, preferred_element_type=jnp.float32)
        d_wvalue = jnp.einsum("nd,nq->dq", normed, d_value_low, preferred_element_type=jnp.float32)
        d_normed = jnp.einsum(
            "nq,dq->nd", d_query_low, back_query, preferred_element_type=jnp.float32
        )
        d_normed = d_normed + jnp.einsum(
            "nq,dq->nd", d_key_low, back_key, preferred_element_type=jnp.float32
        )
        d_normed = d_normed + jnp.einsum(
            "nq,dq->nd", d_value_low, back_value, preferred_element_type=jnp.float32
        )
        _, norm_one_pull = jax.vjp(norm_apply, stream, back_gain_one.astype(jnp.float32))
        d_stream, d_gain_one = norm_one_pull(d_normed)
        d_input = (d_middle + d_stream).astype(jnp.bfloat16)
        terms = (d_gain_one, d_wquery, d_wkey, d_wvalue, d_wout, d_gain_two, d_wgate, d_wup, d_down)
        totals = tuple((before_sum + term for before_sum, term in zip(totals, terms)))
        return (totals, (result, d_input))

    zero_grads = (
        jnp.zeros((D,), jnp.float32),
        jnp.zeros((D, H * HD), jnp.float32),
        jnp.zeros((D, KVH * HD), jnp.float32),
        jnp.zeros((D, KVH * HD), jnp.float32),
        jnp.zeros((H * HD, D), jnp.float32),
        jnp.zeros((D,), jnp.float32),
        jnp.zeros((D, FF), jnp.float32),
        jnp.zeros((D, FF), jnp.float32),
        jnp.zeros((FF, D), jnp.float32),
    )
    totals, (outputs, d_tokens) = lax.scan(micro_step, zero_grads, (tokens, lengths, cotangent))
    (
        sum_gain_one,
        sum_query,
        sum_key,
        sum_value,
        sum_out,
        sum_gain_two,
        sum_gate,
        sum_up,
        sum_down,
    ) = totals
    gain_one_all, gain_two_all = lax.psum((sum_gain_one, sum_gain_two), ("dp", "ctx"))
    dp_width = D // lax.axis_size("dp")
    dp_start = lax.axis_index("dp") * dp_width
    share_gain_one = lax.dynamic_slice_in_dim(gain_one_all, dp_start, dp_width, 0)
    share_gain_two = lax.dynamic_slice_in_dim(gain_two_all, dp_start, dp_width, 0)
    ctx_parts = (
        lax.psum_scatter(
            sum_query.astype(jnp.bfloat16), "ctx", scatter_dimension=1, tiled=True
        ).astype(jnp.float32),
        lax.psum_scatter(
            sum_key.astype(jnp.bfloat16), "ctx", scatter_dimension=1, tiled=True
        ).astype(jnp.float32),
        lax.psum_scatter(
            sum_value.astype(jnp.bfloat16), "ctx", scatter_dimension=1, tiled=True
        ).astype(jnp.float32),
        lax.psum_scatter(
            sum_out.astype(jnp.bfloat16), "ctx", scatter_dimension=0, tiled=True
        ).astype(jnp.float32),
        lax.psum_scatter(
            sum_gate.astype(jnp.bfloat16), "ctx", scatter_dimension=1, tiled=True
        ).astype(jnp.float32),
        lax.psum_scatter(
            sum_up.astype(jnp.bfloat16), "ctx", scatter_dimension=1, tiled=True
        ).astype(jnp.float32),
        lax.psum_scatter(
            sum_down.astype(jnp.bfloat16), "ctx", scatter_dimension=0, tiled=True
        ).astype(jnp.float32),
    )
    dp_parts = (
        lax.psum_scatter(
            ctx_parts[0].astype(jnp.bfloat16), "dp", scatter_dimension=0, tiled=True
        ).astype(jnp.float32),
        lax.psum_scatter(
            ctx_parts[1].astype(jnp.bfloat16), "dp", scatter_dimension=0, tiled=True
        ).astype(jnp.float32),
        lax.psum_scatter(
            ctx_parts[2].astype(jnp.bfloat16), "dp", scatter_dimension=0, tiled=True
        ).astype(jnp.float32),
        lax.psum_scatter(
            ctx_parts[3].astype(jnp.bfloat16), "dp", scatter_dimension=1, tiled=True
        ).astype(jnp.float32),
        lax.psum_scatter(
            ctx_parts[4].astype(jnp.bfloat16), "dp", scatter_dimension=0, tiled=True
        ).astype(jnp.float32),
        lax.psum_scatter(
            ctx_parts[5].astype(jnp.bfloat16), "dp", scatter_dimension=0, tiled=True
        ).astype(jnp.float32),
        lax.psum_scatter(
            ctx_parts[6].astype(jnp.bfloat16), "dp", scatter_dimension=1, tiled=True
        ).astype(jnp.float32),
    )
    whole = (
        lax.all_gather(dp_parts[0].astype(jnp.bfloat16), "ctx", axis=1, tiled=True).astype(
            jnp.float32
        ),
        lax.all_gather(dp_parts[1].astype(jnp.bfloat16), "ctx", axis=1, tiled=True).astype(
            jnp.float32
        ),
        lax.all_gather(dp_parts[2].astype(jnp.bfloat16), "ctx", axis=1, tiled=True).astype(
            jnp.float32
        ),
        lax.all_gather(dp_parts[3].astype(jnp.bfloat16), "ctx", axis=0, tiled=True).astype(
            jnp.float32
        ),
        lax.all_gather(dp_parts[4].astype(jnp.bfloat16), "ctx", axis=1, tiled=True).astype(
            jnp.float32
        ),
        lax.all_gather(dp_parts[5].astype(jnp.bfloat16), "ctx", axis=1, tiled=True).astype(
            jnp.float32
        ),
        lax.all_gather(dp_parts[6].astype(jnp.bfloat16), "ctx", axis=0, tiled=True).astype(
            jnp.float32
        ),
    )
    return (
        outputs,
        d_tokens,
        share_gain_one,
        whole[0],
        whole[1],
        whole[2],
        whole[3],
        share_gain_two,
        whole[4],
        whole[5],
        whole[6],
    )


def solution(mesh):
    return jax.shard_map(
        local,
        mesh=mesh,
        in_specs=(
            P("dp", "ctx", None),
            P("dp", None),
            P("dp"),
            P("dp", None),
            P("dp", None),
            P("dp", None),
            P(None, "dp"),
            P("dp"),
            P("dp", None),
            P("dp", None),
            P(None, "dp"),
            P("dp", "ctx", None),
        ),
        out_specs=(
            P("dp", "ctx", None),
            P("dp", "ctx", None),
            P("dp"),
            P("dp", None),
            P("dp", None),
            P("dp", None),
            P(None, "dp"),
            P("dp"),
            P("dp", None),
            P("dp", None),
            P(None, "dp"),
        ),
        check_vma=False,
    )
```

profile of v0, /device:TPU:0, one launch (start us, length us, event | category | flops | bytes accessed | tf_op | source)
XLA Modules:
  0.0 1448.5 jit_solution(7800385191914006201)
XLA Ops:
  9.9 739.7 %while.93 = (s32[]{:T(128)}, f32[960]{0:T(1024)}, f32[960,960]{1,0:T(8,128)}, f32[960,320]{0,1:T(8,128)}, f32[960,320]{0,1:T(8,128)}, /*index=5*/f32[960,960]{1,...) while((s32[]{:T(128)}, f32[960]{0:T(1024)}, ...), condition=%wide.region_20.21_spmd.clone, body=%wide.region_0.20_spmd.clone.sunk | while | flops 25610287104 | bytes 786864896 | solution.py:351
  20.0 15.2 %all-reduce.17 = (bf16[960]{0:T(1024)(128)(2,1)S(1)}, bf16[960]{0:T(1024)(128)(2,1)S(1)}) all-reduce(bf16[960]{0:T(1024)(128)(2,1)S(1)} %dynamic-update-slice.6, bf16[960]{0:T(1024)(128)(2,1)S(1)} %dynamic-update-slice.7), channel_id=1, replica_groups=mesh['dp'=8,'ctx'=4] {'dp'}, use_global_device_ids=true, to_apply=%add.4 | all-reduce | flops 1920 | bytes 7680 | tf_op jit(solution)/shard_map/while
  47.4 22.2 %all_gather.84 = bf16[1536,320]{0,1:T(8,128)(2,1)S(1)} all-gather(bf16[384,320]{0,1:T(8,128)(2,1)S(1)} %bitcast.478), channel_id=1, replica_groups=mesh['dp'=8,'ctx'=4] {'ctx'}, dimensions={0}, use_global_device_ids=true | all-gather | bytes 1228800 | tf_op jit(solution)/shard_map/while/body/eval_jaxpr/all_gather | solution.py:129
  86.8 22.2 %all_gather.86 = bf16[1536,320]{0,1:T(8,128)(2,1)} all-gather(bf16[384,320]{0,1:T(8,128)(2,1)S(1)} %convolution_convert_fusion.4), channel_id=1, replica_groups=mesh['dp'=8,'ctx'=4] {'ctx'}, dimensions={0}, use_global_device_ids=true | all-gather | bytes 1228800 | tf_op jit(solution)/shard_map/while/body/eval_jaxpr/all_gather | solution.py:130
  121.1 42.6 %while.94 = (s32[]{:T(128)}, f32[5,3,384]{2,1,0:T(4,128)S(1)}, f32[5,3,384]{2,1,0:T(4,128)S(1)}, s32[4,384]{1,0:T(4,128)S(1)}, s32[384]{0:T(512)S(1)}, /*index=5...) while((s32[]{:T(128)}, f32[5,3,384]{2,1,0:T(4,128)S(1)}, ...), condition=%wide.region_5.5_spmd.clone, body=%wide.region_2.4_spmd.clone.sunk | while | flops 299069568 | bytes 19432064 | solution.py:158
  163.7 20.9 %while.95 = (s32[]{:T(128)}, f32[384,5,3,64]{0,3,2,1:T(8,128)}, s32[4,384]{1,0:T(4,128)S(1)}, s32[384]{0:T(512)S(1)}, s32[4,384]{1,0:T(4,128)S(1)}, /*index=5*/s...) while((s32[]{:T(128)}, f32[384,5,3,64]{0,3,2,1:T(8,128)}, ...), condition=%wide.region_7.7_spmd.clone, body=%wide.region_6.6_spmd.clone.sunk | while | flops 578469888 | bytes 4547723 | solution.py:179
  226.7 26.6 %while.96 = (s32[]{:T(128)}, f32[5,3,384]{2,1,0:T(4,128)S(1)}, s32[4,384]{1,0:T(4,128)S(1)}, s32[384]{0:T(512)S(1)}, s32[4,384]{1,0:T(4,128)S(1)}, /*index=5*/s3...) while((s32[]{:T(128)}, f32[5,3,384]{2,1,0:T(4,128)S(1)}, ...), condition=%wide.region_12.12_spmd.clone, body=%wide.region_10.11_spmd.clone.sunk | while | flops 579950208 | bytes 20107408 | solution.py:250
  253.4 55.2 %while.97 = (s32[]{:T(128)}, f32[384,5,3,64]{0,3,2,1:T(8,128)S(1)}, bf16[4,384,320]{1,2,0:T(8,128)(2,1)}, bf16[4,384,320]{1,2,0:T(8,128)(2,1)}, s32[4,384]{1,0:T...) while((s32[]{:T(128)}, f32[384,5,3,64]{0,3,2,1:T(8,128)S(1)}, ...), condition=%wide.region_14.14_spmd.clone, body=%wide.region_13.13_spmd.clone.sunk | while | flops 1435066368 | bytes 65996488 | solution.py:297
  349.1 21.2 %reduce-scatter.65.cloned.1.call-done = bf16[384,320]{1,0:T(8,128)(2,1)} async-done(((bf16[1536,320]{1,0:T(8,128)(2,1)}), bf16[384,320]{1,0:T(8,128)(2,1)}) %reduce-scatter.65.cloned.1.call-update) | async-done | bytes 245776 | tf_op jit(solution)/shard_map/while
  388.9 13.5 all-reduce.17
  413.8 21.0 %all_gather.84 = bf16[1536,320]{0,1:T(8,128)(2,1)S(1)} all-gather(bf16[384,320]{0,1:T(8,128)(2,1)S(1)} %bitcast.478), channel_id=1, replica_groups=mesh['dp'=8,'ctx'=4] {'ctx'}, dimensions={0}, use_global_device_ids=true | all-gather | bytes 1228800 | tf_op jit(solution)/shard_map/while/body/eval_jaxpr/all_gather | solution.py:129
  451.9 21.9 %all_gather.86 = bf16[1536,320]{0,1:T(8,128)(2,1)} all-gather(bf16[384,320]{0,1:T(8,128)(2,1)S(1)} %convolution_convert_fusion.4), channel_id=1, replica_groups=mesh['dp'=8,'ctx'=4] {'ctx'}, dimensions={0}, use_global_device_ids=true | all-gather | bytes 1228800 | tf_op jit(solution)/shard_map/while/body/eval_jaxpr/all_gather | solution.py:130
  485.9 42.6 %while.94 = (s32[]{:T(128)}, f32[5,3,384]{2,1,0:T(4,128)S(1)}, f32[5,3,384]{2,1,0:T(4,128)S(1)}, s32[4,384]{1,0:T(4,128)S(1)}, s32[384]{0:T(512)S(1)}, /*index=5...) while((s32[]{:T(128)}, f32[5,3,384]{2,1,0:T(4,128)S(1)}, ...), condition=%wide.region_5.5_spmd.clone, body=%wide.region_2.4_spmd.clone.sunk | while | flops 299069568 | bytes 19432064 | solution.py:158
  528.5 20.9 %while.95 = (s32[]{:T(128)}, f32[384,5,3,64]{0,3,2,1:T(8,128)}, s32[4,384]{1,0:T(4,128)S(1)}, s32[384]{0:T(512)S(1)}, s32[4,384]{1,0:T(4,128)S(1)}, /*index=5*/s...) while((s32[]{:T(128)}, f32[384,5,3,64]{0,3,2,1:T(8,128)}, ...), condition=%wide.region_7.7_spmd.clone, body=%wide.region_6.6_spmd.clone.sunk | while | flops 578469888 | bytes 4547723 | solution.py:179
  591.6 26.6 %while.96 = (s32[]{:T(128)}, f32[5,3,384]{2,1,0:T(4,128)S(1)}, s32[4,384]{1,0:T(4,128)S(1)}, s32[384]{0:T(512)S(1)}, s32[4,384]{1,0:T(4,128)S(1)}, /*index=5*/s3...) while((s32[]{:T(128)}, f32[5,3,384]{2,1,0:T(4,128)S(1)}, ...), condition=%wide.region_12.12_spmd.clone, body=%wide.region_10.11_spmd.clone.sunk | while | flops 579950208 | bytes 20107408 | solution.py:250
  618.2 55.2 %while.97 = (s32[]{:T(128)}, f32[384,5,3,64]{0,3,2,1:T(8,128)S(1)}, bf16[4,384,320]{1,2,0:T(8,128)(2,1)}, bf16[4,384,320]{1,2,0:T(8,128)(2,1)}, s32[4,384]{1,0:T...) while((s32[]{:T(128)}, f32[384,5,3,64]{0,3,2,1:T(8,128)S(1)}, ...), condition=%wide.region_14.14_spmd.clone, body=%wide.region_13.13_spmd.clone.sunk | while | flops 1435066368 | bytes 65996488 | solution.py:297
  720.9 14.0 reduce-scatter.65.cloned.1.call-done
  806.0 34.2 %reduce-scatter.49.cloned.1.call-done = bf16[240,960]{1,0:T(8,128)(2,1)} async-done(((bf16[960,960]{1,0:T(8,128)(2,1)}), bf16[240,960]{1,0:T(8,128)(2,1)}) %reduce-scatter.49.cloned.1.call-update) | async-done | bytes 460816
  842.3 40.9 %reduce-scatter.47.cloned.1.call-done = bf16[240,960]{1,0:T(8,128)(2,1)} async-done(((bf16[960,960]{1,0:T(8,128)(2,1)}), bf16[240,960]{1,0:T(8,128)(2,1)}) %reduce-scatter.47.cloned.1.call-update) | async-done | bytes 460816 | tf_op jit(solution)/shard_map/reduce_scatter | solution.py:378
  885.3 93.0 %reduce-scatter.53.cloned.1.call-done = bf16[640,960]{1,0:T(8,128)(2,1)} async-done(((bf16[2560,960]{1,0:T(8,128)(2,1)}), bf16[640,960]{1,0:T(8,128)(2,1)}) %reduce-scatter.53.cloned.1.call-update) | async-done | bytes 1228816
  980.8 94.1 %reduce-scatter.55.cloned.1.call-done = bf16[640,960]{1,0:T(8,128)(2,1)} async-done(((bf16[2560,960]{1,0:T(8,128)(2,1)}), bf16[640,960]{1,0:T(8,128)(2,1)}) %reduce-scatter.55.cloned.1.call-update) | async-done | bytes 1228816
  1077.4 93.9 %reduce-scatter.57.cloned.1.call-done = bf16[640,960]{1,0:T(8,128)(2,1)} async-done(((bf16[2560,960]{1,0:T(8,128)(2,1)}), bf16[640,960]{1,0:T(8,128)(2,1)}) %reduce-scatter.57.cloned.1.call-update) | async-done | bytes 1228816
  1173.7 41.0 %all-reduce.14 = (f32[960]{0:T(1024)S(1)}, f32[960]{0:T(1024)S(1)}) all-reduce(f32[960]{0:T(1024)S(1)} %copy-done.54, f32[960]{0:T(1024)S(1)} %copy-done.51), channel_id=1, replica_groups=mesh['dp'=8,'ctx'=4] {'dp','ctx'}, use_global_device_ids=true, to_apply=%region_21.22 | all-reduce | flops 1920 | bytes 15360 | tf_op jit(solution)/shard_map/psum | solution.py:363
  1265.8 13.9 all_gather.63
  1280.6 21.4 %reduce-scatter.51.cloned.1.call-done = bf16[120,240]{1,0:T(8,128)(2,1)} async-done(((bf16[960,240]{1,0:T(8,128)(2,1)}), bf16[120,240]{1,0:T(8,128)(2,1)}) %reduce-scatter.51.cloned.1.call-update) | async-done | bytes 57616
  1302.9 13.9 all_gather.66
  1317.6 24.7 %reduce-scatter.59.cloned.1.call-done = bf16[120,640]{1,0:T(8,128)(2,1)} async-done(((bf16[960,640]{1,0:T(8,128)(2,1)}), bf16[120,640]{1,0:T(8,128)(2,1)}) %reduce-scatter.59.cloned.1.call-update) | async-done | bytes 153616
  1342.3 17.2 %all_gather.67 = bf16[120,2560]{1,0:T(8,128)(2,1)S(1)} all-gather(bf16[120,640]{1,0:T(8,128)(2,1)} %reduce-scatter.59.cloned.1.call-done), channel_id=1, replica_groups=mesh['dp'=8,'ctx'=4] {'ctx'}, dimensions={1}, use_global_device_ids=true | all-gather | bytes 768000 | tf_op jit(solution)/shard_map/all_gather | solution.py:427
  1360.6 22.1 %reduce-scatter.61.cloned.1.call-done = bf16[120,640]{1,0:T(8,128)(2,1)} async-done(((bf16[960,640]{1,0:T(8,128)(2,1)}), bf16[120,640]{1,0:T(8,128)(2,1)}) %reduce-scatter.61.cloned.1.call-update) | async-done | bytes 153616
  1382.7 17.2 %all_gather.68 = bf16[120,2560]{1,0:T(8,128)(2,1)S(1)} all-gather(bf16[120,640]{1,0:T(8,128)(2,1)} %reduce-scatter.61.cloned.1.call-done), channel_id=1, replica_groups=mesh['dp'=8,'ctx'=4] {'ctx'}, dimensions={1}, use_global_device_ids=true | all-gather | bytes 768000 | tf_op jit(solution)/shard_map/all_gather | solution.py:430
  1401.1 21.4 %reduce-scatter.63.cloned.1.call-done = bf16[640,120]{0,1:T(8,128)(2,1)} async-done(((bf16[640,960]{0,1:T(8,128)(2,1)}), bf16[640,120]{0,1:T(8,128)(2,1)}) %reduce-scatter.63.cloned.1.call-update) | async-done | bytes 153616
  1422.5 17.2 %all_gather.69 = bf16[2560,120]{0,1:T(8,128)(2,1)S(1)} all-gather(bf16[640,120]{0,1:T(8,128)(2,1)} %reduce-scatter.63.cloned.1.call-done), channel_id=1, replica_groups=mesh['dp'=8,'ctx'=4] {'ctx'}, dimensions={0}, use_global_device_ids=true | all-gather | bytes 768000 | tf_op jit(solution)/shard_map/all_gather | solution.py:433
  (756 shorter events, 700.3 us)
Async XLA Ops:
  9.9 104.1 %all-gather.14.cloned.1.call-start = ((), (), s32[]{:S(2)}) async-start(), calls=%async_computation.27 | async-start | bytes 2211840 | tf_op jit(solution)/shard_map/while/body/eval_jaxpr/all_gather | solution.py:93
  10.7 176.7 %all-gather.16.cloned.1.call-start = ((), (), s32[]{:S(2)}) async-start(), calls=%async_computation.28 | async-start | bytes 2211840 | tf_op jit(solution)/shard_map/while/body/eval_jaxpr/all_gather | solution.py:96
  11.4 180.3 %all-gather.20.cloned.1.call-start = ((), (), s32[]{:S(2)}) async-start(), calls=%async_computation.30 | async-start | bytes 5529600 | tf_op jit(solution)/shard_map/while/body/eval_jaxpr/all_gather | solution.py:201
  12.2 186.8 %all-gather.18.cloned.1.call-start = ((), (), s32[]{:S(2)}) async-start(), calls=%async_computation.29 | async-start | bytes 5529600 | tf_op jit(solution)/shard_map/while/body/eval_jaxpr/all_gather | solution.py:98
  12.7 192.7 %all-gather.22.cloned.1.call-start = ((), (), s32[]{:S(2)}) async-start(), calls=%async_computation.31 | async-start | bytes 5529600 | tf_op jit(solution)/shard_map/while/body/eval_jaxpr/all_gather | solution.py:99
  13.3 332.6 %reduce-scatter.67.cloned.1.call-start = ((), (), s32[]{:S(2)}) async-start(), calls=%async_computation.33 | async-start | bytes 1474560 | tf_op jit(solution)/shard_map/while
  18.2 99.6 %copy-start.45 = (f32[384]{0:T(512)}, f32[384]{0:T(512)S(1)}, u32[]{:S(2)}) copy-start(f32[384]{0:T(512)S(1)} %fusion.292) | copy-start | bytes 4612 | tf_op jit(solution)/shard_map/while
  310.9 59.3 %reduce-scatter.65.cloned.1.call-start = ((), (), s32[]{:S(2)}) async-start(), calls=%async_computation.32 | async-start | bytes 1474560 | tf_op jit(solution)/shard_map/while
  378.8 100.0 %all-gather.14.cloned.1.call-start = ((), (), s32[]{:S(2)}) async-start(), calls=%async_computation.27 | async-start | bytes 2211840 | tf_op jit(solution)/shard_map/while/body/eval_jaxpr/all_gather | solution.py:93
  379.6 172.6 %all-gather.16.cloned.1.call-start = ((), (), s32[]{:S(2)}) async-start(), calls=%async_computation.28 | async-start | bytes 2211840 | tf_op jit(solution)/shard_map/while/body/eval_jaxpr/all_gather | solution.py:96
  380.3 176.3 %all-gather.20.cloned.1.call-start = ((), (), s32[]{:S(2)}) async-start(), calls=%async_computation.30 | async-start | bytes 5529600 | tf_op jit(solution)/shard_map/while/body/eval_jaxpr/all_gather | solution.py:201
  380.9 182.9 %all-gather.18.cloned.1.call-start = ((), (), s32[]{:S(2)}) async-start(), calls=%async_computation.29 | async-start | bytes 5529600 | tf_op jit(solution)/shard_map/while/body/eval_jaxpr/all_gather | solution.py:98
  381.6 188.7 %all-gather.22.cloned.1.call-start = ((), (), s32[]{:S(2)}) async-start(), calls=%async_computation.31 | async-start | bytes 5529600 | tf_op jit(solution)/shard_map/while/body/eval_jaxpr/all_gather | solution.py:99
  382.2 335.5 %reduce-scatter.67.cloned.1.call-start = ((), (), s32[]{:S(2)}) async-start(), calls=%async_computation.33 | async-start | bytes 1474560 | tf_op jit(solution)/shard_map/while
  387.1 95.6 %copy-start.45 = (f32[384]{0:T(512)}, f32[384]{0:T(512)S(1)}, u32[]{:S(2)}) copy-start(f32[384]{0:T(512)S(1)} %fusion.292) | copy-start | bytes 4612 | tf_op jit(solution)/shard_map/while
  675.8 59.1 %reduce-scatter.65.cloned.1.call-start = ((), (), s32[]{:S(2)}) async-start(), calls=%async_computation.32 | async-start | bytes 1474560 | tf_op jit(solution)/shard_map/while
  749.6 55.9 %reduce-scatter.43.cloned.1.call-start = ((), (), s32[]{:S(2)}) async-start(), calls=%async_computation.15 | async-start | bytes 819200 | tf_op jit(solution)/shard_map/reduce_scatter | solution.py:372
  752.0 53.5 %reduce-scatter.45.cloned.1.call-start = ((), (), s32[]{:S(2)}) async-start(), calls=%async_computation.16 | async-start | bytes 819200 | tf_op jit(solution)/shard_map/reduce_scatter | solution.py:375
  753.0 87.2 %reduce-scatter.49.cloned.1.call-start = ((), (), s32[]{:S(2)}) async-start(), calls=%async_computation.18 | async-start | bytes 2457600
  758.0 125.2 %reduce-scatter.47.cloned.1.call-start = ((), (), s32[]{:S(2)}) async-start(), calls=%async_computation.17 | async-start | bytes 2457600 | tf_op jit(solution)/shard_map/reduce_scatter | solution.py:378
  761.8 216.6 %reduce-scatter.53.cloned.1.call-start = ((), (), s32[]{:S(2)}) async-start(), calls=%async_computation.20 | async-start | bytes 6553600
  776.3 298.5 %reduce-scatter.55.cloned.1.call-start = ((), (), s32[]{:S(2)}) async-start(), calls=%async_computation.21 | async-start | bytes 6553600
  790.8 380.4 %reduce-scatter.57.cloned.1.call-start = ((), (), s32[]{:S(2)}) async-start(), calls=%async_computation.22 | async-start | bytes 6553600
  805.3 423.1 %all-reduce.20.cloned.1.call-start = ((), (), s32[]{:S(2)}) async-start(), calls=%async_computation.26 | async-start | bytes 655360
  805.9 458.9 %reduce-scatter.41.cloned.1.call-start = ((), (), s32[]{:S(2)}) async-start(), calls=%async_computation.14 | async-start | bytes 552960 | tf_op jit(solution)/shard_map/reduce_scatter | solution.py:392
  842.3 459.7 %reduce-scatter.51.cloned.1.call-start = ((), (), s32[]{:S(2)}) async-start(), calls=%async_computation.19 | async-start | bytes 552960
  885.2 457.1 %reduce-scatter.59.cloned.1.call-start = ((), (), s32[]{:S(2)}) async-start(), calls=%async_computation.23 | async-start | bytes 1382400
  980.7 402.0 %reduce-scatter.61.cloned.1.call-start = ((), (), s32[]{:S(2)}) async-start(), calls=%async_computation.24 | async-start | bytes 1382400
  1077.3 96.4 %copy-start.51 = (f32[960]{0:T(1024)S(1)}, f32[960]{0:T(1024)}, u32[]{:S(2)}) copy-start(f32[960]{0:T(1024)} %get-tuple-element.487) | copy-start | bytes 11524
  1077.3 96.4 %copy-start.54 = (f32[960]{0:T(1024)S(1)}, f32[960]{0:T(1024)}, u32[]{:S(2)}) copy-start(f32[960]{0:T(1024)} %get-tuple-element.482) | copy-start | bytes 11524
  1077.3 138.6 %copy-start.66 = (u32[32]{0:T(128)S(1)}, u32[32]{0:T(128)}, u32[]{:S(2)}) copy-start(u32[32]{0:T(128)} %get-tuple-element.2203) | copy-start | bytes 388
  1077.3 345.2 %reduce-scatter.63.cloned.1.call-start = ((), (), s32[]{:S(2)}) async-start(), calls=%async_computation.25 | async-start | bytes 1382400
  (141 other events, 1265.3 us)
Sparse Core Ops, SparseCore 0:
  12.7 31.0 all-gather.13
  46.2 27.7 all-gather.15
  75.9 39.7 all-gather.19
  117.4 39.7 all-gather.17
  158.9 39.7 all-gather.21
  311.0 28.3 reduce-scatter.66
  342.3 27.8 reduce-scatter.64
  381.5 26.6 all-gather.13
  410.7 28.1 all-gather.15
  440.6 39.7 all-gather.19
  482.3 39.7 all-gather.17
  523.8 39.7 all-gather.21
  675.9 28.2 reduce-scatter.66
  707.0 27.8 reduce-scatter.64
Sparse Core Ops, SparseCore 1:
  752.9 21.0 reduce-scatter.42
  776.7 21.0 reduce-scatter.44
  800.0 40.1 reduce-scatter.48
  842.6 40.6 reduce-scatter.46
  885.5 92.8 reduce-scatter.52
  980.6 94.2 reduce-scatter.54
  1077.0 94.2 reduce-scatter.56
  1174.2 54.2 all-reduce.19
  1232.0 32.8 reduce-scatter.40
  1268.6 33.4 reduce-scatter.50
  1305.8 36.5 reduce-scatter.58
  1346.2 36.5 reduce-scatter.60
  1385.9 36.5 reduce-scatter.62
where the time goes:
time: 1450 us
  waiting for transfers between devices  506 us (35%)
  matrix products  376 us (26%)
  blocking collectives  302 us (21%)
  local copies, waits for them, and re-layouts  130 us (9%)
  other arithmetic  103 us (7%)
  between operations  16.7 us (1%)
    unnamed x22, waiting for transfers between devices  417 us
    dot_general x24, matrix products, block_scores(): jnp.einsum('nkgd,ckd->kgnc', queries, key_block, preferred_element_type=j...  98.8 us
    while x316, local copies, waits for them, and re-layouts  58.2 us
    all_gather x2, blocking collectives, micro_step(): lax.all_gather(values_own, 'ctx', axis=0, tiled=True)  44.1 us
    unnamed x23, local copies, waits for them, and re-layouts  43.3 us
    all_gather x2, blocking collectives, micro_step(): lax.all_gather(keys_own, 'ctx', axis=0, tiled=True)  43.1 us
    reduce_sum x8, other arithmetic, find_update(): jnp.sum(expos, -1)  43.1 us
    while x18, waiting for transfers between devices  41.5 us
  transfers between devices with their start and end apart: 27, of which 13 were waited for; matrix products, arithmetic and copies ran while one was open for 25% of the time, Pallas kernels for 0%

commit v1 on v0

v1 whole, which is shorter than its diff:
```python
import functools
import math

import jax
import jax.numpy as jnp
from jax import lax
from jax.experimental import pallas as pl
from jax.experimental.pallas import tpu as pltpu
from jax.sharding import PartitionSpec as P

D = 960
H = 15
KVH = 5
HD = 64
FF = 2560
GROUPS = H // KVH
QW = H * HD
KW = KVH * HD

NORM_EPSILON = 1e-05
ROPE_BASE = 10000.0
MASKED_SCORE = -1e30
F32 = jnp.float32
BF16 = jnp.bfloat16


def dot(left, right, dims):
    return lax.dot_general(left, right, (dims, ((), ())), preferred_element_type=F32)


def fill_bias(info_ref, bias, tok):
    pack = pl.program_id(0)
    own = info_ref[pack, 0]
    first_end = info_ref[pack, 1]
    second_end = info_ref[pack, 2]
    query = own * tok + lax.broadcasted_iota(jnp.int32, (tok, tok), 1)
    start = jnp.where(
        query >= second_end, second_end, jnp.where(query >= first_end, first_end, 0)
    )

    def one(block, carry):
        key = block * tok + lax.broadcasted_iota(jnp.int32, (tok, tok), 0)
        allowed = (key >= start) & (key <= query)
        bias[block] = jnp.where(allowed, 0.0, MASKED_SCORE)
        return carry

    lax.fori_loop(0, own + 1, one, 0)


def forward_kernel(tok, info_ref, q_ref, kv_ref, attn_ref, lse_ref, bias):
    own = info_ref[pl.program_id(0), 0]

    @pl.when(pl.program_id(1) == 0)
    def _():
        fill_bias(info_ref, bias, tok)

    def one(step, carry):
        block = own - step
        keys = kv_ref[block, 0].T
        values = kv_ref[block, 1]
        mask = bias[block]
        state = []
        for g in range(GROUPS):
            top, total, accum = carry[g]
            scores = dot(keys, q_ref[g * HD : (g + 1) * HD, :], ((1,), (0,))) + mask
            new_top = jnp.maximum(top, jnp.max(scores, 0, keepdims=True))
            scaled = jnp.exp(top - new_top)
            expos = jnp.exp(scores - new_top)
            total = total * scaled + jnp.sum(expos, 0, keepdims=True)
            accum = accum * scaled + dot(values, expos.astype(BF16), ((1,), (0,)))
            state.append((new_top, total, accum))
        return tuple(state)

    begin = tuple(
        (
            jnp.full((1, tok), MASKED_SCORE, F32),
            jnp.zeros((1, tok), F32),
            jnp.zeros((HD, tok), F32),
        )
        for _ in range(GROUPS)
    )
    final = lax.fori_loop(0, own + 1, one, begin)
    for g in range(GROUPS):
        top, total, accum = final[g]
        attn_ref[g * HD : (g + 1) * HD, :] = (accum / total).astype(BF16)
        lse_ref[0, g : g + 1, :] = top + jnp.log(total)


def backward_kernel(
    tok, count, info_ref, q_ref, kv_ref, do_ref, attn_ref, lse_ref, dq_ref, dkv_ref, bias
):
    own = info_ref[pl.program_id(0), 0]

    @pl.when(pl.program_id(1) == 0)
    def _():
        fill_bias(info_ref, bias, tok)

    dq_ref[...] = jnp.zeros_like(dq_ref)
    queries = [q_ref[g * HD : (g + 1) * HD, :] for g in range(GROUPS)]
    d_attn = [do_ref[g * HD : (g + 1) * HD, :] for g in range(GROUPS)]
    queries_t = [value.T for value in queries]
    d_attn_t = [value.T for value in d_attn]
    delta = [
        jnp.sum(
            d_attn[g].astype(F32) * attn_ref[g * HD : (g + 1) * HD, :].astype(F32),
            0,
            keepdims=True,
        )
        for g in range(GROUPS)
    ]

    def one(block, carry):
        keys = kv_ref[block, 0]
        keys_t = keys.T
        values_t = kv_ref[block, 1].T
        mask = bias[block]
        dk = jnp.zeros((tok, HD), F32)
        dv = jnp.zeros((tok, HD), F32)
        for g in range(GROUPS):
            scores = dot(keys_t, queries[g], ((1,), (0,))) + mask
            probs = jnp.exp(scores - lse_ref[0, g : g + 1, :])
            d_probs = dot(values_t, d_attn[g], ((1,), (0,)))
            d_scores = (probs * (d_probs - delta[g])).astype(BF16)
            dv = dv + dot(probs.astype(BF16), d_attn_t[g], ((1,), (0,)))
            dk = dk + dot(d_scores, queries_t[g], ((1,), (0,)))
            dq_ref[g * HD : (g + 1) * HD, :] += dot(keys, d_scores, ((1,), (0,)))
        dkv_ref[block, 0] = dk.T.astype(BF16)
        dkv_ref[block, 1] = dv.T.astype(BF16)
        return carry

    def blank(block, carry):
        dkv_ref[block] = jnp.zeros(dkv_ref.shape[1:], BF16)
        return carry

    lax.fori_loop(0, own + 1, one, 0)
    lax.fori_loop(own + 1, count, blank, 0)


def attention_specs(tok, count):
    return (
        pl.BlockSpec(memory_space=pltpu.SMEM),
        pl.BlockSpec((GROUPS * HD, tok), lambda b, k: (k, b)),
        pl.BlockSpec((count, 2, HD, tok), lambda b, k: (0, 0, k, b)),
        pl.BlockSpec((1, GROUPS, tok), lambda b, k: (k, 0, b)),
    )


PARAMS = dict(vmem_limit_bytes=48 * 1024 * 1024)


def attend_forward(info, queries, kv, packs, tok, count):
    smem, rows, pairs, stats = attention_specs(tok, count)
    pairs_done = packs * H * tok * tok * count
    return pl.pallas_call(
        functools.partial(forward_kernel, tok),
        grid=(packs, KVH),
        in_specs=[smem, rows, pairs],
        out_specs=[rows, stats],
        out_shape=[
            jax.ShapeDtypeStruct((QW, packs * tok), BF16),
            jax.ShapeDtypeStruct((KVH, GROUPS, packs * tok), F32),
        ],
        scratch_shapes=[pltpu.VMEM((count, tok, tok), F32)],
        compiler_params=pltpu.CompilerParams(**PARAMS),
        cost_estimate=pl.CostEstimate(
            flops=16 * HD * pairs_done, bytes_accessed=10_000_000, transcendentals=pairs_done
        ),
        name="attend_forward",
    )(info, queries, kv)


def attend_backward(info, queries, kv, d_attn, attn, lse, packs, tok, count):
    smem, rows, pairs, stats = attention_specs(tok, count)
    pairs_done = packs * H * tok * tok * count
    return pl.pallas_call(
        functools.partial(backward_kernel, tok, count),
        grid=(packs, KVH),
        in_specs=[smem, rows, pairs, rows, rows, stats],
        out_specs=[rows, pairs],
        out_shape=[
            jax.ShapeDtypeStruct((QW, packs * tok), F32),
            jax.ShapeDtypeStruct((count, 2, KW, packs * tok), BF16),
        ],
        scratch_shapes=[pltpu.VMEM((count, tok, tok), F32)],
        compiler_params=pltpu.CompilerParams(**PARAMS),
        cost_estimate=pl.CostEstimate(
            flops=40 * HD * pairs_done, bytes_accessed=20_000_000, transcendentals=pairs_done
        ),
        name="attend_backward",
    )(info, queries, kv, d_attn, attn, lse)


def rotate(values, cosine, sine):
    tokens = values.shape[-1]
    pairs = values.reshape(-1, 2, HD // 2, tokens)
    first, second = pairs[:, 0], pairs[:, 1]
    return jnp.stack(
        [first * cosine - second * sine, second * cosine + first * sine], 1
    ).reshape(values.shape)


def norm_back(d_normed, values, inverse, gain):
    d_gain = jnp.sum(d_normed * values * inverse, 0)
    scaled = d_normed * gain
    d_values = inverse * scaled - values * (inverse * inverse * inverse) * jnp.mean(
        values * scaled, -1, keepdims=True
    )
    return d_gain, d_values


def local(
    tokens,
    lengths,
    gain_attn,
    w_query,
    w_key,
    w_value,
    w_out,
    gain_ffn,
    w_gate,
    w_up,
    w_down,
    cotangent,
):
    packs, tok, _ = tokens.shape
    rows = packs * tok
    count = lax.axis_size("ctx")
    own = lax.axis_index("ctx")

    gains = lax.all_gather(jnp.stack([gain_attn, gain_ffn]), "dp", axis=1, tiled=True).astype(F32)
    gain_one, gain_two = gains[0], gains[1]
    full_qkv = lax.all_gather(
        jnp.concatenate([w_query, w_key, w_value], 1), "dp", axis=0, tiled=True
    )
    full_out_t = lax.all_gather(w_out.T, "dp", axis=0, tiled=True)
    full_gate_up = lax.all_gather(jnp.concatenate([w_gate, w_up], 1), "dp", axis=0, tiled=True)
    full_down_t = lax.all_gather(w_down.T, "dp", axis=0, tiled=True)

    first_end = lengths[:, 0:1]
    second_end = first_end + lengths[:, 1:2]
    places = own * tok + jnp.arange(tok, dtype=jnp.int32)[None, :]
    begin = jnp.where(places >= second_end, second_end, jnp.where(places >= first_end, first_end, 0))
    positions = (places - begin).reshape(rows).astype(F32)
    half = HD // 2
    frequency = ROPE_BASE ** (-jnp.arange(half, dtype=F32) / half)
    angles = frequency[:, None] * positions[None, :]
    cosine, sine = jnp.cos(angles), jnp.sin(angles)
    info = jnp.concatenate(
        [jnp.full_like(first_end, own), first_end, second_end, jnp.zeros_like(first_end)], 1
    )

    stream = tokens.reshape(rows, D).astype(F32)
    inverse_one = lax.rsqrt(jnp.mean(stream * stream, -1, keepdims=True) + NORM_EPSILON)
    normed = (stream * inverse_one * gain_one).astype(BF16)
    qkv = dot(full_qkv, normed, ((0,), (1,)))
    queries = rotate(qkv[:QW], cosine, sine).astype(BF16) * jnp.asarray(1 / math.sqrt(HD), BF16)
    keys = rotate(qkv[QW : QW + KW], cosine, sine).astype(BF16)
    values = qkv[QW + KW :].astype(BF16)
    kv = lax.all_gather(jnp.stack([keys, values]), "ctx", axis=0, tiled=False)

    attn, lse = attend_forward(info, queries, kv, packs, tok, count)

    middle = stream + dot(attn, full_out_t, ((0,), (1,)))
    inverse_two = lax.rsqrt(jnp.mean(middle * middle, -1, keepdims=True) + NORM_EPSILON)
    normed_two = (middle * inverse_two * gain_two).astype(BF16)
    gate_up = dot(normed_two, full_gate_up, ((1,), (0,)))
    gate, up = gate_up[:, :FF], gate_up[:, FF:]
    sigma = jax.nn.sigmoid(gate)
    silu = gate * sigma
    hidden = (silu * up).astype(BF16)

    cot = cotangent.reshape(rows, D)
    d_hidden = dot(cot, full_down_t, ((1,), (0,)))
    d_gate = (d_hidden * up * sigma * (1.0 + gate * (1.0 - sigma))).astype(BF16)
    d_up = (d_hidden * silu).astype(BF16)

    def reduced(term):
        part = lax.psum_scatter(term, "dp", scatter_dimension=0, tiled=True)
        return lax.psum(part, "ctx").astype(F32)

    g_down = reduced(dot(cot, hidden, ((0,), (0,))).astype(BF16))
    g_gate = reduced(dot(normed_two, d_gate, ((0,), (0,))).astype(BF16))
    g_up = reduced(dot(normed_two, d_up, ((0,), (0,))).astype(BF16))

    output = (middle + dot(hidden, full_down_t, ((1,), (1,)))).astype(BF16)

    d_normed_two = dot(d_gate, full_gate_up[:, :FF], ((1,), (1,))) + dot(
        d_up, full_gate_up[:, FF:], ((1,), (1,))
    )
    d_gain_two, d_middle_norm = norm_back(d_normed_two, middle, inverse_two, gain_two)
    d_middle = cot.astype(F32) + d_middle_norm
    d_mixed = d_middle.astype(BF16)
    d_attn = dot(full_out_t, d_mixed, ((0,), (1,))).astype(BF16)

    dq, dkv_terms = attend_backward(info, queries, kv, d_attn, attn, lse, packs, tok, count)
    g_out = reduced(dot(d_mixed, attn, ((0,), (1,))).astype(BF16))
    dkv = lax.psum_scatter(dkv_terms, "ctx", scatter_dimension=0, tiled=False)

    d_query = rotate(dq * (1 / math.sqrt(HD)), cosine, -sine).astype(BF16)
    d_key = rotate(dkv[0].astype(F32), cosine, -sine).astype(BF16)
    d_qkv = jnp.concatenate([d_query, d_key, dkv[1]], 0)
    g_qkv = reduced(dot(normed, d_qkv, ((0,), (1,))).astype(BF16))
    d_normed = dot(d_qkv, full_qkv, ((0,), (1,)))
    d_gain_one, d_stream = norm_back(d_normed, stream, inverse_one, gain_one)
    d_tokens = (d_middle + d_stream).astype(BF16)

    d_gains = lax.psum(jnp.stack([d_gain_one, d_gain_two]), ("dp", "ctx"))
    width = gain_attn.shape[0]
    share = lax.dynamic_slice_in_dim(d_gains, lax.axis_index("dp") * width, width, 1)

    return (
        output.reshape(packs, tok, D),
        d_tokens.reshape(packs, tok, D),
        share[0],
        g_qkv[:, :QW],
        g_qkv[:, QW : QW + KW],
        g_qkv[:, QW + KW :],
        g_out.T,
        share[1],
        g_gate,
        g_up,
        g_down.T,
    )


def solution(mesh):
    return jax.shard_map(
        local,
        mesh=mesh,
        in_specs=(
            P("dp", "ctx", None),
            P("dp", None),
            P("dp"),
            P("dp", None),
            P("dp", None),
            P("dp", None),
            P(None, "dp"),
            P("dp"),
            P("dp", None),
            P("dp", None),
            P(None, "dp"),
            P("dp", "ctx", None),
        ),
        out_specs=(
            P("dp", "ctx", None),
            P("dp", "ctx", None),
            P("dp"),
            P("dp", None),
            P("dp", None),
            P("dp", None),
            P(None, "dp"),
            P("dp"),
            P("dp", None),
            P("dp", None),
            P(None, "dp"),
        ),
        check_vma=False,
    )
```

time: 1450 us -> 830 us (0.57)
  matrix products: 376 us -> 104 us
  blocking collectives: 302 us -> 53.6 us
  local copies, waits for them, and re-layouts: 130 us -> 27.1 us
  other arithmetic: 103 us -> 20.3 us
  waiting for transfers between devices: 506 us -> 570 us
  Pallas kernels: 0 us -> 33.5 us
    unnamed x22 -> x13, waiting for transfers between devices: 417 us -> 50.8 us
    dot_general x114 -> x14, matrix products: 376 us -> 104 us  [dot(): lax.dot_general(left, right, (dims, ((), ())), preferred_element_type=F32)]
    reduce_scatter x4 -> x5, waiting for transfers between devices: 47.7 us -> 293 us  [the longest x4 213 us: reduced(): part = lax.psum_scatter(term, 'dp', scatter_dimension=0, tiled=True)]
    all_gather x15 -> x1, blocking collectives: 232 us -> 10.2 us  [local(): lax.all_gather(jnp.stack([gain_attn, gain_ffn]), 'dp', axis=1, tiled=True)]
    all_gather x10 -> x5, waiting for transfers between devices: 0.05 us -> 185 us  [the longest x1 69.7 us: local(): kv = lax.all_gather(jnp.stack([keys, values]), 'ctx', axis=0, tiled=False)]
    while x316 -> x0, local copies, waits for them, and re-layouts: 58.2 us -> none
    reduce_sum x10 -> x1, other arithmetic: 43.5 us -> 1.69 us  [local(): jnp.mean(stream * stream, -1, keepdims=True) + NORM_EPSILON]
    while x18 -> x0, waiting for transfers between devices: 41.5 us -> none
  transfers between devices with their start and end apart: 27 -> 12, of which waited for: 13 -> 12; matrix products, arithmetic and copies ran while one was open for 25% -> 11% of each run, Pallas kernels for 0% -> 2%
where the time goes in v1:
time: 830 us; the launch traced here: 824 us
  waiting for transfers between devices  570 us (69%)
  matrix products  104 us (13%)
  blocking collectives  53.6 us (6%)
  Pallas kernels  33.5 us (4%)
  local copies, waits for them, and re-layouts  27.1 us (3%)
  other arithmetic  20.3 us (2%)
  between operations  14.9 us (2%)
    reduce_scatter x4, waiting for transfers between devices, reduced(): part = lax.psum_scatter(term, 'dp', scatter_dimension=0, tiled=True)  213 us
    dot_general x14, matrix products, dot(): lax.dot_general(left, right, (dims, ((), ())), preferred_element_type=F32)  104 us
    reduce_scatter x1, waiting for transfers between devices, local(): dkv = lax.psum_scatter(dkv_terms, 'ctx', scatter_dimension=0, tiled=False)  80.2 us
    all_gather x1, waiting for transfers between devices, local(): kv = lax.all_gather(jnp.stack([keys, values]), 'ctx', axis=0, tiled=False)  69.7 us
    all_gather x1, waiting for transfers between devices, local(): lax.all_gather(jnp.concatenate([w_gate, w_up], 1), 'dp', axis=0, tiled=True)  55.7 us
    unnamed x13, waiting for transfers between devices  50.8 us
    psum x1, blocking collectives, local(): d_gains = lax.psum(jnp.stack([d_gain_one, d_gain_two]), ('dp', 'ctx'))  43.3 us
    psum x1, waiting for transfers between devices, reduced(): return lax.psum(part, 'ctx').astype(F32)  41.3 us
  transfers between devices with their start and end apart: 12, of which 12 were waited for; matrix products, arithmetic and copies ran while one was open for 11% of the time, Pallas kernels for 2%

profile of v1, /device:TPU:0, one launch (start us, length us, event | category | flops | bytes accessed | tf_op | source)
XLA Modules:
  0.0 824.3 jit_solution(3658154030982967652)
XLA Ops:
  13.4 10.2 %all-gather.1 = bf16[8,120,2]{1,2,0:T(2,128)(2,1)S(1)} all-gather(bf16[1,120,2]{1,2,0:T(2,128)(2,1)S(1)} %maximum_bitcast_fusion), channel_id=1, replica_groups=mesh['dp'=8,'ctx'=4] {'dp'}, dimensions={0}, use_global_device_ids=true | all-gather | bytes 4320 | tf_op jit(solution)/shard_map/all_gather | solution.py:230
  26.9 19.5 %all-gather.8.cloned.1.call-done = bf16[960,1600]{1,0:T(8,128)(2,1)} async-done(((bf16[120,1600]{1,0:T(8,128)(2,1)}), bf16[960,1600]{1,0:T(8,128)(2,1)}) %all-gather.8.cloned.1.call-update) | async-done | bytes 3072016 | tf_op jit(solution)/shard_map/all_gather | solution.py:232
  46.4 4.9 fusion.20
  51.4 2.2 copy-done.5
  61.8 69.7 %all-gather.16.cloned.1.call-done = bf16[8,320,768]{2,1,0:T(8,128)(2,1)} async-done(((bf16[2,320,768]{2,1,0:T(8,128)(2,1)}), bf16[8,320,768]{2,1,0:T(8,128)(2,1)}) %all-gather.16.cloned.1.call-update) | async-done | bytes 3932176 | tf_op jit(solution)/shard_map/all_gather | solution.py:259
  131.5 15.4 %attend_forward.1 = (bf16[960,768]{1,0:T(8,128)(2,1)S(1)}, f32[5,3,768]{2,1,0:T(4,128)S(1)}) custom-call(s32[2,4]{1,0:T(2,128)S(1)} %add_add_fusion.info_ref, bf16[960,768]{1,0:T(8,128)(2,1)S(1)} %bitcast.73, bf16[4,2,320,768]{3,2,1,0:T(8,128)(2,1)} %bitcast.109), custom_call_target="tpu_custom_call" | custom-call | flops 18119393280 | bytes 10000000 | tf_op jit(solution)/shard_map/attend_forward/pallas_call | solution.py:154
  146.9 13.1 %all-gather.10.cloned.1.call-done = bf16[960,960]{1,0:T(8,128)(2,1)} async-done(((bf16[120,960]{1,0:T(8,128)(2,1)}), bf16[960,960]{1,0:T(8,128)(2,1)}) %all-gather.10.cloned.1.call-update) | async-done | bytes 1843216 | tf_op jit(solution)/shard_map/all_gather | solution.py:235
  160.1 4.1 multiply_reduce_fusion.4
  167.2 55.7 %all-gather.12.cloned.1.call-done = bf16[960,5120]{1,0:T(8,128)(2,1)} async-done(((bf16[120,5120]{1,0:T(8,128)(2,1)}), bf16[960,5120]{1,0:T(8,128)(2,1)}) %all-gather.12.cloned.1.call-update) | async-done | bytes 9830416 | tf_op jit(solution)/shard_map/all_gather | solution.py:236
  222.9 14.6 %fusion.25 = f32[768,5120]{1,0:T(8,128)} fusion(bf16[768,960]{0,1:T(8,128)(2,1)} %multiply_convert_fusion.3, bf16[960,5120]{1,0:T(8,128)(2,1)} %all-gather.12.cloned.1.call-done), kind=kOutput, calls=%fused_computation.87 | convolution fusion | flops 7549747200 | bytes 27033600 | tf_op jit(solution)/shard_map/dot_general | solution.py:28
  237.5 26.9 %all-gather.14.cloned.1.call-done = bf16[960,2560]{1,0:T(8,128)(2,1)} async-done(((bf16[120,2560]{1,0:T(8,128)(2,1)}), bf16[960,2560]{1,0:T(8,128)(2,1)}) %all-gather.14.cloned.1.call-update) | async-done | bytes 4915216 | tf_op jit(solution)/shard_map/all_gather | solution.py:237
  264.4 15.6 %multiply_convert_fusion.1 = (bf16[768,2560]{1,0:T(8,128)(2,1)S(1)}, bf16[768,2560]{1,0:T(8,128)(2,1)}, bf16[768,2560]{1,0:T(8,128)(2,1)}) fusion(f32[768,5120]{1,0:T(8,128)} %fusion.25, bf16[768,960]{0,1:T(8,128)(2,1)} %bitcast.82, bf16[960,2560]{1,0:T(8,128)(2,1)} %all-gather.14.cloned.1.call-done), kind=kOutput, calls=%fused_computation.1 | convolution fusion | flops 3804364800 | bytes 33914880 | tf_op jit(solution)/shard_map/dot_general | solution.py:28
  280.0 9.2 %fusion.1 = f32[768,960]{0,1:T(8,128)} fusion(bf16[768,2560]{1,0:T(8,128)(2,1)} %get-tuple-element.75, bf16[960,5120]{1,0:T(8,128)(2,1)S(1)} %copy-done.30), kind=kOutput, calls=%fused_computation.8 | convolution fusion | flops 3774873600 | bytes 11796480 | tf_op jit(solution)/shard_map/dot_general | solution.py:28
  289.2 6.3 multiply_reduce_fusion
  298.9 18.1 %attend_backward.1 = (f32[960,768]{1,0:T(8,128)}, bf16[4,2,320,768]{3,2,1,0:T(8,128)(2,1)}) custom-call(s32[2,4]{1,0:T(2,128)S(1)} %add_add_fusion.info_ref, bf16[960,768]{1,0:T(8,128)(2,1)S(1)} %bitcast.74, bf16[4,2,320,768]{3,2,1,0:T(8,128)(2,1)} %bitcast.110, bf16[960,768]{1,0:T(8,128)(2,1)S(1)} %fusion.10.do_ref, ...), custom_call_target="tpu_custom_call" | custom-call | flops 45298483200 | bytes 20000000 | tf_op jit(solution)/shard_map/attend_backward/pallas_call | solution.py:175
  317.1 4.9 convolution_convert_fusion.4
  322.2 8.2 convolution_convert_fusion.2
  330.4 7.8 convolution_convert_fusion.1
  339.6 7.7 fusion.5
  351.8 80.2 %reduce-scatter.9.cloned.1.call-done = bf16[1,2,320,768]{3,2,1,0:T(8,128)(2,1)} async-done(((bf16[4,2,320,768]{3,2,1,0:T(8,128)(2,1)}), bf16[1,2,320,768]{3,2,1,0:T(8,128)(2,1)}) %reduce-scatter.9.cloned.1.call-update) | async-done | bytes 983056 | tf_op jit(solution)/shard_map/reduce_scatter | solution.py:297
  434.2 4.6 convolution_convert_fusion.3
  439.1 37.1 %reduce-scatter.11.cloned.1.call-done = bf16[120,960]{1,0:T(8,128)(2,1)} async-done(((bf16[960,960]{1,0:T(8,128)(2,1)}), bf16[120,960]{1,0:T(8,128)(2,1)}) %reduce-scatter.11.cloned.1.call-update) | async-done | bytes 230416 | tf_op jit(solution)/shard_map/reduce_scatter | solution.py:278
  476.1 58.8 %reduce-scatter.13.cloned.1.call-done = bf16[120,2560]{1,0:T(8,128)(2,1)} async-done(((bf16[960,2560]{1,0:T(8,128)(2,1)}), bf16[120,2560]{1,0:T(8,128)(2,1)}) %reduce-scatter.13.cloned.1.call-update) | async-done | bytes 614416 | tf_op jit(solution)/shard_map/reduce_scatter | solution.py:278
  534.9 58.5 %reduce-scatter.15.cloned.1.call-done = bf16[120,2560]{1,0:T(8,128)(2,1)} async-done(((bf16[960,2560]{1,0:T(8,128)(2,1)}), bf16[120,2560]{1,0:T(8,128)(2,1)}) %reduce-scatter.15.cloned.1.call-update) | async-done | bytes 614416 | tf_op jit(solution)/shard_map/reduce_scatter | solution.py:278
  593.4 58.6 %reduce-scatter.17.cloned.1.call-done = bf16[120,2560]{1,0:T(8,128)(2,1)} async-done(((bf16[960,2560]{1,0:T(8,128)(2,1)}), bf16[120,2560]{1,0:T(8,128)(2,1)}) %reduce-scatter.17.cloned.1.call-update) | async-done | bytes 614416 | tf_op jit(solution)/shard_map/reduce_scatter | solution.py:278
  652.0 50.0 %reduce-scatter.19.cloned.1.call-done = bf16[120,1600]{1,0:T(8,128)(2,1)} async-done(((bf16[960,1600]{1,0:T(8,128)(2,1)}), bf16[120,1600]{1,0:T(8,128)(2,1)}) %reduce-scatter.19.cloned.1.call-update) | async-done | bytes 384016
  702.1 9.7 %add_convert_fusion.1 = bf16[768,960]{0,1:T(8,128)(2,1)} fusion(f32[768,960]{0,1:T(8,128)} %copy-done.2, bf16[768,2560]{1,0:T(8,128)(2,1)} %get-tuple-element.76, bf16[960,2560]{1,0:T(8,128)(2,1)} %all-gather.14.cloned.1.call-done), kind=kOutput, calls=%fused_computation.23 | convolution fusion | flops 3776348160 | bytes 13271040 | tf_op jit(solution)/shard_map/dot_general | solution.py:28
  711.8 4.5 multiply_reduce_fusion.1
  716.3 43.3 %psum.42 = f32[2,960]{1,0:T(2,128)S(1)} all-reduce(f32[2,960]{1,0:T(2,128)S(1)} %pad_maximum_fusion.8), channel_id=1, replica_groups=mesh['dp'=8,'ctx'=4] {'dp','ctx'}, use_global_device_ids=true, to_apply=%region_7.8 | all-reduce | flops 1920 | bytes 15360 | tf_op jit(solution)/shard_map/psum | solution.py:307
  760.3 3.8 add_convert_fusion
  766.0 41.3 %all-reduce.4.cloned.1.call-done = (bf16[120,1600]{1,0:T(8,128)(2,1)}, bf16[960,120]{0,1:T(8,128)(2,1)}, bf16[120,2560]{1,0:T(8,128)(2,1)}, bf16[120,2560]{1,0:T(8,128)(2,1)}, bf16[2560,120]{0,1:T(8,128)(2,1)}) async-done(((bf16[120,1600]{1,0:T(8,128)(2,1)}, bf16[960,120]{0,1:T(8,128)(2,1)}, bf16[120,2560]{1,0:T(8,128)(2,1)}, bf16[120,2560]{1,0:T(8,128)(2,1)}, bf16[2560,120]{0,1:T(8,128)(2,1)}), ...) | async-done | bytes 2457616 | tf_op jit(solution)/shard_map/psum | solution.py:279
  810.2 2.3 convert_element_type.134
  (158 shorter events, 42.5 us)
Async XLA Ops:
  7.2 39.3 %all-gather.8.cloned.1.call-start = ((), (), s32[]{:S(2)}) async-start(), calls=%async_computation.6 | async-start | bytes 3594240 | tf_op jit(solution)/shard_map/all_gather | solution.py:232
  11.1 120.5 %all-gather.16.cloned.1.call-start = ((), (), s32[]{:S(2)}) async-start(), calls=%async_computation.15 | async-start | bytes 4915200 | tf_op jit(solution)/shard_map/all_gather | solution.py:259
  12.7 12.7 %copy-start.29 = (s32[2,3]{1,0:T(2,128)S(1)}, s32[2,3]{1,0:T(2,128)}, u32[]{:S(2)}) copy-start(s32[2,3]{1,0:T(2,128)} %param.13) | copy-start | bytes 76
  13.0 38.4 %copy-start = (f32[2,120,8,384]{3,2,0,1:T(8,128)}, f32[2,120,8,384]{3,2,0,1:T(8,128)S(1)}, u32[]{:S(2)}) copy-start(f32[2,120,8,384]{3,2,0,1:T(8,128)S(1)} %copy.66) | copy-start | bytes 8847364
  25.4 25.9 %copy-start.25 = (f32[768]{0:T(1024)}, f32[768]{0:T(1024)S(1)}, u32[]{:S(2)}) copy-start(f32[768]{0:T(1024)S(1)} %rsqrt.26) | copy-start | bytes 9220
  25.8 25.5 %copy-start.27 = (f32[1,960]{1,0:T(1,128)}, f32[1,960]{1,0:T(1,128)S(1)}, u32[]{:S(2)}) copy-start(f32[1,960]{1,0:T(1,128)S(1)} %get-tuple-element.90) | copy-start | bytes 11524
  26.9 32.4 %copy-start.9 = (f32[32,768]{1,0:T(8,128)}, f32[32,768]{1,0:T(8,128)S(1)}, u32[]{:S(2)}) copy-start(f32[32,768]{1,0:T(8,128)S(1)} %get-tuple-element.93) | copy-start | bytes 294916
  54.9 105.1 %all-gather.10.cloned.1.call-start = ((), (), s32[]{:S(2)}) async-start(), calls=%async_computation.7 | async-start | bytes 2211840 | tf_op jit(solution)/shard_map/all_gather | solution.py:235
  55.9 167.0 %all-gather.12.cloned.1.call-start = ((), (), s32[]{:S(2)}) async-start(), calls=%async_computation.8 | async-start | bytes 11059200 | tf_op jit(solution)/shard_map/all_gather | solution.py:236
  57.1 207.3 %all-gather.14.cloned.1.call-start = ((), (), s32[]{:S(2)}) async-start(), calls=%async_computation.9 | async-start | bytes 5529600 | tf_op jit(solution)/shard_map/all_gather | solution.py:237
  57.7 374.3 %reduce-scatter.9.cloned.1.call-start = ((), (), s32[]{:S(2)}) async-start(), calls=%async_computation.10 | async-start | bytes 4915200 | tf_op jit(solution)/shard_map/reduce_scatter | solution.py:297
  264.4 15.6 %copy-start.30 = (bf16[960,5120]{1,0:T(8,128)(2,1)S(1)}, bf16[960,5120]{1,0:T(8,128)(2,1)}, u32[]{:S(2)}) copy-start(bf16[960,5120]{1,0:T(8,128)(2,1)} %all-gather.12.cloned.1.call-done) | copy-start | bytes 29491204
  280.0 9.2 %copy-start.35 = (bf16[768,2560]{1,0:T(8,128)(2,1)}, bf16[768,2560]{1,0:T(8,128)(2,1)S(1)}, u32[]{:S(2)}) copy-start(bf16[768,2560]{1,0:T(8,128)(2,1)S(1)} %get-tuple-element.74) | copy-start | bytes 11796484
  280.0 9.2 %copy-start.3 = (f32[768,960]{0,1:T(8,128)S(1)}, f32[768,960]{0,1:T(8,128)}, u32[]{:S(2)}) copy-start(f32[768,960]{0,1:T(8,128)} %copy-done.2) | copy-start | bytes 8847364
  289.2 6.4 copy-start.6
  317.1 5.1 copy-start.14
  317.1 159.0 %reduce-scatter.11.cloned.1.call-start = ((), (), s32[]{:S(2)}) async-start(), calls=%async_computation.11 | async-start | bytes 2211840 | tf_op jit(solution)/shard_map/reduce_scatter | solution.py:278
  322.1 212.8 %reduce-scatter.13.cloned.1.call-start = ((), (), s32[]{:S(2)}) async-start(), calls=%async_computation.12 | async-start | bytes 5529600 | tf_op jit(solution)/shard_map/reduce_scatter | solution.py:278
  330.4 263.0 %reduce-scatter.15.cloned.1.call-start = ((), (), s32[]{:S(2)}) async-start(), calls=%async_computation.13 | async-start | bytes 5529600 | tf_op jit(solution)/shard_map/reduce_scatter | solution.py:278
  338.3 313.7 %reduce-scatter.17.cloned.1.call-start = ((), (), s32[]{:S(2)}) async-start(), calls=%async_computation.14 | async-start | bytes 5529600 | tf_op jit(solution)/shard_map/reduce_scatter | solution.py:278
  347.4 354.7 %reduce-scatter.19.cloned.1.call-start = ((), (), s32[]{:S(2)}) async-start(), calls=%async_computation.16 | async-start | bytes 3594240
  351.8 82.3 %copy-start.1 = (f32[2,120,8,384]{3,2,0,1:T(8,128)S(1)}, f32[2,120,8,384]{3,2,0,1:T(8,128)}, u32[]{:S(2)}) copy-start(f32[2,120,8,384]{3,2,0,1:T(8,128)} %copy-done) | copy-start | bytes 8847364
  351.8 82.3 %copy-start.26 = (f32[768]{0:T(1024)S(1)}, f32[768]{0:T(1024)}, u32[]{:S(2)}) copy-start(f32[768]{0:T(1024)} %copy-done.25) | copy-start | bytes 9220
  351.8 82.3 %copy-start.28 = (f32[1,960]{1,0:T(1,128)S(1)}, f32[1,960]{1,0:T(1,128)}, u32[]{:S(2)}) copy-start(f32[1,960]{1,0:T(1,128)} %copy-done.27) | copy-start | bytes 11524
  438.8 368.4 %all-reduce.4.cloned.1.call-start = ((), (), s32[]{:S(2)}) async-start(), calls=%async_computation.17 | async-start | bytes 4976640 | tf_op jit(solution)/shard_map/psum | solution.py:279
  702.1 9.7 %copy-start.13 = (bf16[15,2,32,768]{3,2,1,0:T(8,128)(2,1)S(1)}, bf16[15,2,32,768]{3,2,1,0:T(8,128)(2,1)}, u32[]{:S(2)}) copy-start(bf16[15,2,32,768]{3,2,1,0:T(8,128)(2,1)} %pad_maximum_fusion.1) | copy-start | bytes 4423684
  702.1 9.7 %copy-start.22 = (bf16[320,768]{1,0:T(8,128)(2,1)S(1)}, bf16[320,768]{1,0:T(8,128)(2,1)}, u32[]{:S(2)}) copy-start(bf16[320,768]{1,0:T(8,128)(2,1)} %copy-done.21) | copy-start | bytes 1474564
  702.1 9.7 %copy-start.31 = (bf16[960,1600]{1,0:T(8,128)(2,1)S(1)}, bf16[960,1600]{1,0:T(8,128)(2,1)}, u32[]{:S(2)}) copy-start(bf16[960,1600]{1,0:T(8,128)(2,1)} %all-gather.8.cloned.1.call-done) | copy-start | bytes 9216004
  760.3 3.8 copy-start.15
  807.2 5.2 copy-start.18
  807.2 6.3 copy-start.17
  810.1 6.1 copy-start.24
  (17 other events, 27.3 us)
Sparse Core Ops, SparseCore 0:
  11.2 35.2 all-gather.7
  55.1 76.4 all-gather.15
  134.0 26.0 all-gather.9
  162.4 60.4 all-gather.11
  224.6 39.7 all-gather.13
  317.2 114.7 reduce-scatter.8
  435.4 40.6 reduce-scatter.10
  480.0 54.8 reduce-scatter.12
  538.4 54.8 reduce-scatter.14
  597.1 54.8 reduce-scatter.16
  655.4 46.5 reduce-scatter.18
  704.9 102.3 all-reduce.3

commit v2 on v1

--- a/solution.py
+++ b/solution.py
@@ -38,10 +38,10 @@
         query >= second_end, second_end, jnp.where(query >= first_end, first_end, 0)
     )
 
-    def one(block, carry):
-        key = block * tok + lax.broadcasted_iota(jnp.int32, (tok, tok), 0)
+    def one(slot, carry):
+        key = (own - slot) * tok + lax.broadcasted_iota(jnp.int32, (tok, tok), 0)
         allowed = (key >= start) & (key <= query)
-        bias[block] = jnp.where(allowed, 0.0, MASKED_SCORE)
+        bias[slot] = jnp.where(allowed, 0.0, MASKED_SCORE)
         return carry
 
     lax.fori_loop(0, own + 1, one, 0)
@@ -54,8 +54,7 @@
     def _():
         fill_bias(info_ref, bias, tok)
 
-    def one(step, carry):
-        block = own - step
+    def one(block, carry):
         keys = kv_ref[block, 0].T
         values = kv_ref[block, 1]
         mask = bias[block]
@@ -208,6 +207,40 @@
     return d_gain, d_values
 
 
+ORDER = (0, 2, 4, 6, 1, 3, 5, 7)
+
+
+def swap(value, bit):
+    return lax.ppermute(value, "dp", [(i, i ^ bit) for i in range(8)])
+
+
+def gather_shards(shard):
+    middle = shard.shape[0] // 16 * 8
+    from_x, from_y = swap(shard, 2), swap(shard, 4)
+    diagonal = jnp.concatenate([swap(from_x[:middle], 4), swap(from_y[middle:], 2)], 0)
+    near = (shard, from_x, from_y, diagonal)
+    return jnp.concatenate(near + tuple(swap(part, 1) for part in near), 0)
+
+
+def add(left, right):
+    return (left.astype(F32) + right.astype(F32)).astype(BF16)
+
+
+def reduce_shards(keep, send):
+    columns = keep.shape[1]
+    own = add(keep, swap(send, 1)).reshape(4, -1, columns)
+    split = columns // 256 * 128
+    one = own[:, :, :split]
+    two = own[:, :, split:]
+    from_x = swap(jnp.stack([one[1], one[3]]), 2)
+    from_y = swap(two[2:], 4)
+    last_y = swap(add(one[2], from_x[1]), 4)
+    last_x = swap(add(two[1], from_y[1]), 2)
+    done_one = add(add(one[0], from_x[0]), last_y)
+    done_two = add(add(two[0], from_y[0]), last_x)
+    return jnp.concatenate([done_one, done_two], 1)
+
+
 def local(
     tokens,
     lengths,
@@ -226,15 +259,39 @@
     rows = packs * tok
     count = lax.axis_size("ctx")
     own = lax.axis_index("ctx")
-
-    gains = lax.all_gather(jnp.stack([gain_attn, gain_ffn]), "dp", axis=1, tiled=True).astype(F32)
+    direct = lax.axis_size("dp") == 8
+    width = D // lax.axis_size("dp")
+    half_model = D // 2
+
+    if direct:
+        place = jnp.arange(D, dtype=jnp.int32)
+        shard = jnp.bitwise_xor(
+            jnp.repeat(jnp.asarray(ORDER, jnp.int32), width), lax.axis_index("dp")
+        )
+        chosen = (place[:, None] == (shard * width + place % width)[None, :]).astype(BF16)
+
+    def arrange(value):
+        return dot(value, chosen, ((1,), (0,))).astype(BF16) if direct else value
+
+    def restore(value):
+        return dot(value, chosen, ((1,), (1,))).astype(BF16) if direct else value
+
+    def gathered(value):
+        if direct:
+            return gather_shards(value)
+        return lax.all_gather(value, "dp", axis=0, tiled=True)
+
+    full_qkv = gathered(
+        jnp.concatenate([w_query, w_key, w_value, gain_attn[:, None], gain_ffn[:, None]], 1)
+    )
+    down_out = jnp.concatenate([w_down.T, w_out.T], 1)
+    gate_up = jnp.concatenate([w_gate, w_up], 1)
+    full_qkv, down_out, gate_up = lax.optimization_barrier((full_qkv, down_out, gate_up))
+    full_gate_up = gathered(gate_up)
+    full_down_out = gathered(down_out)
+    full_down_t, full_out_t = full_down_out[:, :FF], full_down_out[:, FF:]
+    gains = full_qkv[:, QW + 2 * KW :].astype(F32).T
     gain_one, gain_two = gains[0], gains[1]
-    full_qkv = lax.all_gather(
-        jnp.concatenate([w_query, w_key, w_value], 1), "dp", axis=0, tiled=True
-    )
-    full_out_t = lax.all_gather(w_out.T, "dp", axis=0, tiled=True)
-    full_gate_up = lax.all_gather(jnp.concatenate([w_gate, w_up], 1), "dp", axis=0, tiled=True)
-    full_down_t = lax.all_gather(w_down.T, "dp", axis=0, tiled=True)
 
     first_end = lengths[:, 0:1]
     second_end = first_end + lengths[:, 1:2]
@@ -249,14 +306,22 @@
         [jnp.full_like(first_end, own), first_end, second_end, jnp.zeros_like(first_end)], 1
     )
 
-    stream = tokens.reshape(rows, D).astype(F32)
+    stream = arrange(tokens.reshape(rows, D)).astype(F32)
+    cot = arrange(cotangent.reshape(rows, D))
     inverse_one = lax.rsqrt(jnp.mean(stream * stream, -1, keepdims=True) + NORM_EPSILON)
     normed = (stream * inverse_one * gain_one).astype(BF16)
     qkv = dot(full_qkv, normed, ((0,), (1,)))
     queries = rotate(qkv[:QW], cosine, sine).astype(BF16) * jnp.asarray(1 / math.sqrt(HD), BF16)
     keys = rotate(qkv[QW : QW + KW], cosine, sine).astype(BF16)
-    values = qkv[QW + KW :].astype(BF16)
-    kv = lax.all_gather(jnp.stack([keys, values]), "ctx", axis=0, tiled=False)
+    values = qkv[QW + KW : QW + 2 * KW].astype(BF16)
+    own_kv = jnp.stack([keys, values])
+    kv = jnp.stack(
+        [own_kv]
+        + [
+            lax.ppermute(own_kv, "ctx", [(i, i + d) for i in range(count - d)])
+            for d in range(1, count)
+        ]
+    )
 
     attn, lse = attend_forward(info, queries, kv, packs, tok, count)
 
@@ -269,18 +334,24 @@
     silu = gate * sigma
     hidden = (silu * up).astype(BF16)
 
-    cot = cotangent.reshape(rows, D)
     d_hidden = dot(cot, full_down_t, ((1,), (0,)))
     d_gate = (d_hidden * up * sigma * (1.0 + gate * (1.0 - sigma))).astype(BF16)
     d_up = (d_hidden * silu).astype(BF16)
 
-    def reduced(term):
-        part = lax.psum_scatter(term, "dp", scatter_dimension=0, tiled=True)
-        return lax.psum(part, "ctx").astype(F32)
-
-    g_down = reduced(dot(cot, hidden, ((0,), (0,))).astype(BF16))
-    g_gate = reduced(dot(normed_two, d_gate, ((0,), (0,))).astype(BF16))
-    g_up = reduced(dot(normed_two, d_up, ((0,), (0,))).astype(BF16))
+    def reduced(left, right, axis, extra=()):
+        def term(part, extra_part):
+            product = dot(part, right, ((0,), (axis,))).astype(BF16)
+            return jnp.concatenate((product,) + extra_part, 1)
+
+        if not direct:
+            return lax.psum_scatter(term(left, extra), "dp", scatter_dimension=0, tiled=True)
+        send = term(left[:, half_model:], tuple(e[half_model:] for e in extra))
+        keep = term(left[:, :half_model], tuple(e[:half_model] for e in extra))
+        return reduce_shards(keep, send)
+
+    p_down = reduced(cot, hidden, 0)
+    p_gate = reduced(normed_two, d_gate, 0)
+    p_up = reduced(normed_two, d_up, 0)
 
     output = (middle + dot(hidden, full_down_t, ((1,), (1,)))).astype(BF16)
 
@@ -293,30 +364,39 @@
     d_attn = dot(full_out_t, d_mixed, ((0,), (1,))).astype(BF16)
 
     dq, dkv_terms = attend_backward(info, queries, kv, d_attn, attn, lse, packs, tok, count)
-    g_out = reduced(dot(d_mixed, attn, ((0,), (1,))).astype(BF16))
-    dkv = lax.psum_scatter(dkv_terms, "ctx", scatter_dimension=0, tiled=False)
+    p_out = reduced(d_mixed, attn, 1)
+    dkv = dkv_terms[0].astype(F32)
+    for d in range(1, count):
+        moved = lax.ppermute(dkv_terms[d], "ctx", [(i + d, i) for i in range(count - d)])
+        dkv = dkv + moved.astype(F32)
 
     d_query = rotate(dq * (1 / math.sqrt(HD)), cosine, -sine).astype(BF16)
-    d_key = rotate(dkv[0].astype(F32), cosine, -sine).astype(BF16)
-    d_qkv = jnp.concatenate([d_query, d_key, dkv[1]], 0)
-    g_qkv = reduced(dot(normed, d_qkv, ((0,), (1,))).astype(BF16))
-    d_normed = dot(d_qkv, full_qkv, ((0,), (1,)))
+    d_key = rotate(dkv[0], cosine, -sine).astype(BF16)
+    d_qkv = jnp.concatenate([d_query, d_key, dkv[1].astype(BF16)], 0)
+    d_normed = dot(
+        jnp.concatenate([d_qkv, jnp.zeros((2, rows), BF16)], 0), full_qkv, ((0,), (1,))
+    )
     d_gain_one, d_stream = norm_back(d_normed, stream, inverse_one, gain_one)
-    d_tokens = (d_middle + d_stream).astype(BF16)
-
-    d_gains = lax.psum(jnp.stack([d_gain_one, d_gain_two]), ("dp", "ctx"))
-    width = gain_attn.shape[0]
-    share = lax.dynamic_slice_in_dim(d_gains, lax.axis_index("dp") * width, width, 1)
+    p_qkv = reduced(
+        normed, d_qkv, 1, (d_gain_one.astype(BF16)[:, None], d_gain_two.astype(BF16)[:, None])
+    )
+    d_tokens = restore((d_middle + d_stream).astype(BF16))
+
+    early = lax.psum((p_down, p_gate, p_up), "ctx")
+    early, p_out, p_qkv = lax.optimization_barrier((early, p_out, p_qkv))
+    late = lax.psum((p_out, p_qkv), "ctx")
+    g_down, g_gate, g_up = (value.astype(F32) for value in early)
+    g_out, g_qkv = (value.astype(F32) for value in late)
 
     return (
-        output.reshape(packs, tok, D),
+        restore(output).reshape(packs, tok, D),
         d_tokens.reshape(packs, tok, D),
-        share[0],
+        g_qkv[:, QW + 2 * KW],
         g_qkv[:, :QW],
         g_qkv[:, QW : QW + KW],
-        g_qkv[:, QW + KW :],
+        g_qkv[:, QW + KW : QW + 2 * KW],
         g_out.T,
-        share[1],
+        g_qkv[:, QW + 2 * KW + 1],
         g_gate,
         g_up,
         g_down.T,

time: 830 us -> 688 us (0.83)
  waiting for transfers between devices: 570 us -> 355 us
  blocking collectives: 53.6 us -> 0 us
  starting transfers between devices: 0.84 us -> 52.1 us
  local copies, waits for them, and re-layouts: 27.1 us -> 61.2 us
  other arithmetic: 20.3 us -> 46.4 us
  matrix products: 104 us -> 119 us
    reduce_scatter x5 -> x0, waiting for transfers between devices: 293 us -> none  [the longest x4 213 us: reduced(): part = lax.psum_scatter(term, 'dp', scatter_dimension=0, tiled=True)]
    ppermute x0 -> x55, waiting for transfers between devices: none -> 262 us  [the longest x3 138 us: local(): lax.ppermute(dkv_terms[d], 'ctx', [(i + d, i) for i in range(count - d)])]
    all_gather x5 -> x0, waiting for transfers between devices: 185 us -> none  [the longest x1 69.7 us: local(): kv = lax.all_gather(jnp.stack([keys, values]), 'ctx', axis=0, tiled=False)]
    ppermute x0 -> x55, starting transfers between devices: none -> 52 us  [the longest x49 38.2 us: swap(): return lax.ppermute(value, 'dp', [(i, i ^ bit) for i in range(8)])]
    psum x1 -> x2, waiting for transfers between devices: 41.3 us -> 93 us  [the longest x1 53.6 us: local(): early = lax.psum((p_down, p_gate, p_up), 'ctx')]
    unnamed x13 -> x2, waiting for transfers between devices: 50.8 us -> 0.03 us
    psum x1 -> x0, blocking collectives: 43.3 us -> none  [local(): d_gains = lax.psum(jnp.stack([d_gain_one, d_gain_two]), ('dp', 'ctx'))]
    unnamed x79 -> x159, local copies, waits for them, and re-layouts: 16.6 us -> 37.9 us
  transfers between devices with their start and end apart: 12 -> 57, of which waited for: 12 -> 28; matrix products, arithmetic and copies ran while one was open for 11% -> 18% of each run, Pallas kernels for 2% -> 2%
where the time goes in v2:
time: 688 us; the launch traced here: 683 us
  waiting for transfers between devices  355 us (52%)
  matrix products  119 us (17%)
  local copies, waits for them, and re-layouts  61.2 us (9%)
  starting transfers between devices  52.1 us (8%)
  other arithmetic  46.4 us (7%)
  Pallas kernels  33.4 us (5%)
  between operations  15.5 us (2%)
    ppermute x3, waiting for transfers between devices, local(): lax.ppermute(dkv_terms[d], 'ctx', [(i + d, i) for i in range(count - d)])  138 us
    dot_general x22, matrix products, dot(): lax.dot_general(left, right, (dims, ((), ())), preferred_element_type=F32)  119 us
    ppermute x49, waiting for transfers between devices, swap(): return lax.ppermute(value, 'dp', [(i, i ^ bit) for i in range(8)])  74.3 us
    psum x1, waiting for transfers between devices, local(): early = lax.psum((p_down, p_gate, p_up), 'ctx')  53.6 us
    ppermute x3, waiting for transfers between devices, local(): lax.ppermute(own_kv, 'ctx', [(i, i + d) for i in range(count - d)])  49.5 us
    psum x1, waiting for transfers between devices, local(): late = lax.psum((p_out, p_qkv), 'ctx')  39.4 us
    ppermute x49, starting transfers between devices, swap(): return lax.ppermute(value, 'dp', [(i, i ^ bit) for i in range(8)])  38.2 us
    unnamed x159, local copies, waits for them, and re-layouts  37.9 us
  transfers between devices with their start and end apart: 57, of which 28 were waited for; matrix products, arithmetic and copies ran while one was open for 18% of the time, Pallas kernels for 2%

profile of v2, /device:TPU:0, one launch (start us, length us, event | category | flops | bytes accessed | tf_op | source)
XLA Modules:
  0.0 682.7 jit_solution(1977346157768267759)
XLA Ops:
  32.7 4.8 collective-permute-done.2
  50.5 4.5 collective-permute-start.9
  63.9 8.8 %collective-permute-done.8 = bf16[2,320,768]{2,1,0:T(8,128)(2,1)S(1)} collective-permute-done((bf16[2,320,768]{2,1,0:T(8,128)(2,1)S(1)}, bf16[2,320,768]{2,1,0:T(8,128)(2,1)S(1)}, u32[]{:S(2)}, u32[]{:S(2)}) %collective-permute-start.8) | collective-permute-done | bytes 983072 | tf_op jit(solution)/shard_map/ppermute | solution.py:321
  72.7 21.1 %collective-permute-done.9 = bf16[2,320,768]{2,1,0:T(8,128)(2,1)S(1)} collective-permute-done((bf16[2,320,768]{2,1,0:T(8,128)(2,1)S(1)}, bf16[2,320,768]{2,1,0:T(8,128)(2,1)S(1)}, u32[]{:S(2)}, u32[]{:S(2)}) %collective-permute-start.9) | collective-permute-done | bytes 983072 | tf_op jit(solution)/shard_map/ppermute | solution.py:321
  93.8 19.6 %collective-permute-done.10 = bf16[2,320,768]{2,1,0:T(8,128)(2,1)S(1)} collective-permute-done((bf16[2,320,768]{2,1,0:T(8,128)(2,1)S(1)}, bf16[2,320,768]{2,1,0:T(8,128)(2,1)S(1)}, u32[]{:S(2)}, u32[]{:S(2)}) %collective-permute-start.10) | collective-permute-done | bytes 983072 | tf_op jit(solution)/shard_map/ppermute | solution.py:321
  116.0 15.4 %attend_forward.1 = (bf16[960,768]{1,0:T(8,128)(2,1)S(1)}, f32[5,3,768]{2,1,0:T(4,128)S(1)}) custom-call(s32[2,4]{1,0:T(2,128)S(1)} %add_add_fusion.info_ref, bf16[960,768]{1,0:T(8,128)(2,1)S(1)} %bitcast.182, bf16[4,2,320,768]{3,2,1,0:T(8,128)(2,1)} %pad_maximum_fusion.kv_ref), custom_call_target="tpu_custom_call" | custom-call | flops 18119393280 | bytes 10000000 | tf_op jit(solution)/shard_map/attend_forward/pallas_call | solution.py:153
  136.9 5.4 collective-permute-done.14
  147.5 7.2 %collective-permute-done.21 = bf16[56,5120]{1,0:T(8,128)(2,1)S(1)} collective-permute-done((bf16[56,5120]{1,0:T(8,128)(2,1)S(1)}, bf16[56,5120]{1,0:T(8,128)(2,1)S(1)}, u32[]{:S(2)}, u32[]{:S(2)}) %collective-permute-start.21) | collective-permute-done | bytes 573472 | tf_op jit(solution)/shard_map/ppermute | solution.py:214
  168.3 3.8 copy-done.33
  172.1 11.1 %fusion.128 = f32[768,5120]{1,0:T(8,128)} fusion(bf16[768,960]{0,1:T(8,128)(2,1)S(1)} %multiply_convert_fusion.3, bf16[960,5120]{1,0:T(8,128)(2,1)S(1)} %constant_dynamic-update-slice_fusion.18), kind=kOutput, calls=%fused_computation.269 | convolution fusion | flops 7549747200 | bytes 27033600 | tf_op jit(solution)/shard_map/dot_general | solution.py:28
  183.2 24.0 %multiply_convert_fusion.1 = (bf16[768,2560]{1,0:T(8,128)(2,1)}, bf16[768,2560]{1,0:T(8,128)(2,1)}, bf16[768,2560]{1,0:T(8,128)(2,1)}) fusion(f32[768,5120]{1,0:T(8,128)} %fusion.128, bf16[960,768]{1,0:T(8,128)(2,1)S(1)} %fusion.49, bf16[960,3520]{1,0:T(8,128)(2,1)} %copy-done.40), kind=kOutput, calls=%fused_computation.1 | convolution fusion | flops 3804364800 | bytes 33914880 | tf_op jit(solution)/shard_map/dot_general | solution.py:28
  207.2 9.3 %fusion.1 = f32[768,960]{0,1:T(8,128)} fusion(bf16[768,2560]{1,0:T(8,128)(2,1)} %get-tuple-element.71, bf16[960,5120]{1,0:T(8,128)(2,1)} %copy-done.33), kind=kOutput, calls=%fused_computation.5 | convolution fusion | flops 3774873600 | bytes 11796480 | tf_op jit(solution)/shard_map/dot_general | solution.py:28
  216.6 7.5 %multiply_reduce_fusion = (bf16[960]{0:T(1024)(128)(2,1)S(1)}, f32[768]{0:T(1024)S(1)}, f32[768,960]{0,1:T(8,128)S(1)}) fusion(f32[768,960]{0,1:T(8,128)S(1)} %get-tuple-element.136, f32[768]{0:T(1024)S(1)} %get-tuple-element.126, f32[960]{0:T(1024)S(1)} %get-tuple-element.61, f32[768,960]{0,1:T(8,128)} %fusion.1, bf16[768,2560]{1,0:T(8,128)(2,1)} %get-tuple-element.70, ...), kind=kOutput, calls=%fused_computation.45 | convolution fusion | flops 3780032768 | bytes 17707904 | tf_op jit(solution)/shard_map/dot_general | solution.py:28
  225.7 3.9 fusion.51.do_ref
  235.1 3.6 convolution_convert_fusion.2
  238.7 18.0 %attend_backward.1 = (f32[960,768]{1,0:T(8,128)}, bf16[4,2,320,768]{3,2,1,0:T(8,128)(2,1)}) custom-call(s32[2,4]{1,0:T(2,128)S(1)} %add_add_fusion.info_ref, bf16[960,768]{1,0:T(8,128)(2,1)S(1)} %bitcast.183, bf16[4,2,320,768]{3,2,1,0:T(8,128)(2,1)} %pad_maximum_fusion.kv_ref, bf16[960,768]{1,0:T(8,128)(2,1)S(1)} %fusion.51.do_ref, ...), custom_call_target="tpu_custom_call" | custom-call | flops 45298483200 | bytes 20000000 | tf_op jit(solution)/shard_map/attend_backward/pallas_call | solution.py:174
  256.7 3.8 broadcast_multiply_fusion
  266.9 13.6 %fusion.48 = bf16[768,960]{0,1:T(8,128)(2,1)} fusion(s32[960]{0:T(1024)S(1)} %copy-done.48, f32[768,960]{0,1:T(8,128)} %copy-done, bf16[768,2560]{1,0:T(8,128)(2,1)} %get-tuple-element.72, bf16[960,3520]{1,0:T(8,128)(2,1)} %copy-done.40), kind=kOutput, calls=%fused_computation.75 | convolution fusion | flops 5193584640 | bytes 13274880 | tf_op jit(solution)/shard_map/dot_general | solution.py:28
  298.1 41.8 %collective-permute-done.27 = bf16[2,320,768]{2,1,0:T(8,128)(2,1)} collective-permute-done((bf16[2,320,768]{2,1,0:T(8,128)(2,1)}, bf16[2,320,768]{2,1,0:T(8,128)(2,1)}, u32[]{:S(2)}, u32[]{:S(2)}) %collective-permute-start.27) | collective-permute-done | bytes 983072 | tf_op jit(solution)/shard_map/ppermute | solution.py:370
  339.9 29.7 %collective-permute-done.28 = bf16[2,320,768]{2,1,0:T(8,128)(2,1)} collective-permute-done((bf16[2,320,768]{2,1,0:T(8,128)(2,1)}, bf16[2,320,768]{2,1,0:T(8,128)(2,1)}, u32[]{:S(2)}, u32[]{:S(2)}) %collective-permute-start.28) | collective-permute-done | bytes 983072 | tf_op jit(solution)/shard_map/ppermute | solution.py:370
  371.2 66.7 %collective-permute-done.29 = bf16[2,320,768]{2,1,0:T(8,128)(2,1)} collective-permute-done((bf16[2,320,768]{2,1,0:T(8,128)(2,1)}, bf16[2,320,768]{2,1,0:T(8,128)(2,1)}, u32[]{:S(2)}, u32[]{:S(2)}) %collective-permute-start.29) | collective-permute-done | bytes 983072 | tf_op jit(solution)/shard_map/ppermute | solution.py:370
  445.2 4.2 fusion.22
  472.7 5.3 add_convert_fusion
  482.0 3.9 add_convert_fusion.1
  489.2 3.8 add_convert_fusion.2
  500.5 9.7 %collective-permute-done.36 = bf16[2,120,1280]{2,1,0:T(8,128)(2,1)} collective-permute-done((bf16[2,120,1280]{2,1,0:T(8,128)(2,1)}, bf16[2,120,1280]{2,1,0:T(8,128)(2,1)}, u32[]{:S(2)}, u32[]{:S(2)}) %collective-permute-start.36) | collective-permute-done | bytes 614432 | tf_op jit(solution)/shard_map/ppermute | solution.py:214
  514.1 9.1 %collective-permute-done.31 = bf16[2,120,1280]{2,1,0:T(8,128)(2,1)S(1)} collective-permute-done((bf16[2,120,1280]{2,1,0:T(8,128)(2,1)}, bf16[2,120,1280]{2,1,0:T(8,128)(2,1)S(1)}, u32[]{:S(2)}, u32[]{:S(2)}) %collective-permute-start.31) | collective-permute-done | bytes 614432 | tf_op jit(solution)/shard_map/ppermute | solution.py:214
  525.9 9.9 %collective-permute-done.37 = bf16[120,1280]{1,0:T(8,128)(2,1)S(1)} collective-permute-done((bf16[120,1280]{1,0:T(8,128)(2,1)S(1)}, bf16[120,1280]{1,0:T(8,128)(2,1)S(1)}, u32[]{:S(2)}, u32[]{:S(2)}) %collective-permute-start.37) | collective-permute-done | bytes 307232 | tf_op jit(solution)/shard_map/ppermute | solution.py:214
  553.5 3.9 collective-permute-done.51
  559.0 4.9 collective-permute-done.53
  570.9 53.6 %all-reduce.7.cloned.1.call-done = (bf16[120,2560]{1,0:T(8,128)(2,1)}, bf16[120,2560]{1,0:T(8,128)(2,1)}, bf16[120,2560]{1,0:T(8,128)(2,1)}) async-done(((bf16[120,2560]{1,0:T(8,128)(2,1)}, bf16[120,2560]{1,0:T(8,128)(2,1)}, bf16[120,2560]{1,0:T(8,128)(2,1)}), (bf16[120,2560]{1,0:T(8,128)(2,1)}, bf16[120,2560]{1,0:T(8,128)(2,1)}, bf16[120,2560]{1,0:T(8,128)(2,1)})) %all-reduce.7.cloned.1.call-update) | async-done | bytes 1843216 | tf_op jit(solution)/shard_map/psum | solution.py:385
  630.2 39.4 %all-reduce.5.cloned.1.call-done = (bf16[120,1602]{0,1:T(8,128)(2,1)}, bf16[960,120]{1,0:T(8,128)(2,1)}) async-done(((bf16[120,1602]{0,1:T(8,128)(2,1)}, bf16[960,120]{1,0:T(8,128)(2,1)}), (bf16[120,1602]{0,1:T(8,128)(2,1)}, bf16[960,120]{1,0:T(8,128)(2,1)})) %all-reduce.5.cloned.1.call-update) | async-done | bytes 614896 | tf_op jit(solution)/shard_map/psum | solution.py:387
  (386 shorter events, 195.6 us)
Async XLA Ops:
  7.2 617.4 %all-reduce.7.cloned.1.call-start = ((), (), s32[]{:S(2)}) async-start(), calls=%async_computation.1 | async-start | bytes 3686400 | tf_op jit(solution)/shard_map/psum | solution.py:385
  12.0 17.2 %collective-permute-start = (bf16[120,1602]{1,0:T(8,128)(2,1)S(1)}, bf16[120,1602]{1,0:T(8,128)(2,1)}, u32[]{:S(2)}, u32[]{:S(2)}) collective-permute-start(bf16[120,1602]{1,0:T(8,128)(2,1)S(1)} %concatenate.62), channel_id=1, source_target_pairs={{0,8},{4,12},{8,0},{12,4},{16,24},{20,28},{24,16},{28,20},{1,9},{5... | collective-permute-start | bytes 1153448 | tf_op jit(solution)/shard_map/ppermute | solution.py:214
  16.5 22.0 %collective-permute-start.4 = (bf16[120,1602]{1,0:T(8,128)(2,1)S(1)}, bf16[120,1602]{1,0:T(8,128)(2,1)}, u32[]{:S(2)}, u32[]{:S(2)}) collective-permute-start(bf16[120,1602]{1,0:T(8,128)(2,1)S(1)} %concatenate.62), channel_id=1, source_target_pairs={{0,4},{4,0},{8,12},{12,8},{16,20},{20,16},{24,28},{28,24},{1,5},{5... | collective-permute-start | bytes 1153448 | tf_op jit(solution)/shard_map/ppermute | solution.py:214
  40.3 21.2 %collective-permute-start.11 = (bf16[120,3520]{1,0:T(8,128)(2,1)S(1)}, bf16[120,3520]{1,0:T(8,128)(2,1)S(1)}, u32[]{:S(2)}, u32[]{:S(2)}) collective-permute-start(bf16[120,3520]{1,0:T(8,128)(2,1)S(1)} %pad_maximum_fusion.8), channel_id=1, source_target_pairs={{0,8},{4,12},{8,0},{12,4},{16,24},{20,28},{24,16},{28,20},{1,9},{5... | collective-permute-start | bytes 2534408 | tf_op jit(solution)/shard_map/ppermute | solution.py:214
  40.7 21.1 %collective-permute-start.12 = (bf16[120,3520]{1,0:T(8,128)(2,1)S(1)}, bf16[120,3520]{1,0:T(8,128)(2,1)S(1)}, u32[]{:S(2)}, u32[]{:S(2)}) collective-permute-start(bf16[120,3520]{1,0:T(8,128)(2,1)S(1)} %pad_maximum_fusion.8), channel_id=1, source_target_pairs={{0,16},{4,20},{8,24},{12,28},{16,0},{20,4},{24,8},{28,12},{1,17},{... | collective-permute-start | bytes 2534408 | tf_op jit(solution)/shard_map/ppermute | solution.py:214
  47.0 25.7 %collective-permute-start.8 = (bf16[2,320,768]{2,1,0:T(8,128)(2,1)S(1)}, bf16[2,320,768]{2,1,0:T(8,128)(2,1)S(1)}, u32[]{:S(2)}, u32[]{:S(2)}) collective-permute-start(bf16[2,320,768]{2,1,0:T(8,128)(2,1)S(1)} %get-tuple-element.115), channel_id=1, source_target_pairs={{0,1},{1,2},{2,3},{4,5},{5,6},{6,7},{8,9},{9,10},{10,11},{12,13},{... | collective-permute-start | bytes 2949128 | tf_op jit(solution)/shard_map/ppermute | solution.py:321
  50.5 43.2 %collective-permute-start.9 = (bf16[2,320,768]{2,1,0:T(8,128)(2,1)S(1)}, bf16[2,320,768]{2,1,0:T(8,128)(2,1)S(1)}, u32[]{:S(2)}, u32[]{:S(2)}) collective-permute-start(bf16[2,320,768]{2,1,0:T(8,128)(2,1)S(1)} %get-tuple-element.115), channel_id=1, source_target_pairs={{0,2},{1,3},{4,6},{5,7},{8,10},{9,11},{12,14},{13,15},{16,18},{17,... | collective-permute-start | bytes 2949128 | tf_op jit(solution)/shard_map/ppermute | solution.py:321
  55.0 58.4 %collective-permute-start.10 = (bf16[2,320,768]{2,1,0:T(8,128)(2,1)S(1)}, bf16[2,320,768]{2,1,0:T(8,128)(2,1)S(1)}, u32[]{:S(2)}, u32[]{:S(2)}) collective-permute-start(bf16[2,320,768]{2,1,0:T(8,128)(2,1)S(1)} %get-tuple-element.115), channel_id=1, source_target_pairs={{0,3},{4,7},{8,11},{12,15},{16,19},{20,23},{24,27},{28,31}} | collective-permute-start | bytes 2949128 | tf_op jit(solution)/shard_map/ppermute | solution.py:321
  61.5 69.9 %collective-permute-start.19 = (bf16[120,5120]{1,0:T(8,128)(2,1)S(1)}, bf16[120,5120]{1,0:T(8,128)(2,1)S(1)}, u32[]{:S(2)}, u32[]{:S(2)}) collective-permute-start(bf16[120,5120]{1,0:T(8,128)(2,1)S(1)} %pad_maximum_fusion.3), channel_id=1, source_target_pairs={{0,8},{4,12},{8,0},{12,4},{16,24},{20,28},{24,16},{28,20},{1,9},{5... | collective-permute-start | bytes 3686408 | tf_op jit(solution)/shard_map/ppermute | solution.py:214
  61.9 72.3 %collective-permute-start.20 = (bf16[120,5120]{1,0:T(8,128)(2,1)S(1)}, bf16[120,5120]{1,0:T(8,128)(2,1)S(1)}, u32[]{:S(2)}, u32[]{:S(2)}) collective-permute-start(bf16[120,5120]{1,0:T(8,128)(2,1)S(1)} %pad_maximum_fusion.3), channel_id=1, source_target_pairs={{0,16},{4,20},{8,24},{12,28},{16,0},{20,4},{24,8},{28,12},{1,17},{... | collective-permute-start | bytes 3686408 | tf_op jit(solution)/shard_map/ppermute | solution.py:214
  72.6 86.3 %collective-permute-start.23 = (bf16[120,5120]{1,0:T(8,128)(2,1)S(1)}, bf16[120,5120]{1,0:T(8,128)(2,1)S(1)}, u32[]{:S(2)}, u32[]{:S(2)}) collective-permute-start(bf16[120,5120]{1,0:T(8,128)(2,1)S(1)} %pad_maximum_fusion.3), channel_id=1, source_target_pairs={{0,4},{4,0},{8,12},{12,8},{16,20},{20,16},{24,28},{28,24},{1,5},{5... | collective-permute-start | bytes 3686408 | tf_op jit(solution)/shard_map/ppermute | solution.py:214
  93.8 50.2 %collective-permute-start.15 = (bf16[120,3520]{1,0:T(8,128)(2,1)S(1)}, bf16[120,3520]{1,0:T(8,128)(2,1)}, u32[]{:S(2)}, u32[]{:S(2)}) collective-permute-start(bf16[120,3520]{1,0:T(8,128)(2,1)S(1)} %pad_maximum_fusion.8), channel_id=1, source_target_pairs={{0,4},{4,0},{8,12},{12,8},{16,20},{20,16},{24,28},{28,24},{1,5},{5... | collective-permute-start | bytes 2534408 | tf_op jit(solution)/shard_map/ppermute | solution.py:214
  113.4 22.0 %collective-permute-start.13 = (bf16[56,3520]{1,0:T(8,128)(2,1)S(1)}, bf16[56,3520]{1,0:T(8,128)(2,1)S(1)}, u32[]{:S(2)}, u32[]{:S(2)}) collective-permute-start(bf16[56,3520]{1,0:T(8,128)(2,1)S(1)} %slice.495), channel_id=1, source_target_pairs={{0,16},{4,20},{8,24},{12,28},{16,0},{20,4},{24,8},{28,12},{1,17},{... | collective-permute-start | bytes 1182728 | tf_op jit(solution)/shard_map/ppermute | solution.py:214
  146.7 17.2 %collective-permute-start.24 = (bf16[120,5120]{1,0:T(8,128)(2,1)S(1)}, bf16[120,5120]{1,0:T(8,128)(2,1)S(1)}, u32[]{:S(2)}, u32[]{:S(2)}) collective-permute-start(bf16[120,5120]{1,0:T(8,128)(2,1)S(1)} %collective-permute-done.19), channel_id=1, source_target_pairs={{0,4},{4,0},{8,12},{12,8},{16,20},{20,16},{24,28},{28,24},{1,5},{5... | collective-permute-start | bytes 3686408 | tf_op jit(solution)/shard_map/ppermute | solution.py:214
  146.9 21.2 %collective-permute-start.25 = (bf16[120,5120]{1,0:T(8,128)(2,1)S(1)}, bf16[120,5120]{1,0:T(8,128)(2,1)S(1)}, u32[]{:S(2)}, u32[]{:S(2)}) collective-permute-start(bf16[120,5120]{1,0:T(8,128)(2,1)S(1)} %collective-permute-done.20), channel_id=1, source_target_pairs={{0,4},{4,0},{8,12},{12,8},{16,20},{20,16},{24,28},{28,24},{1,5},{5... | collective-permute-start | bytes 3686408 | tf_op jit(solution)/shard_map/ppermute | solution.py:214
  262.1 77.8 %collective-permute-start.27 = (bf16[2,320,768]{2,1,0:T(8,128)(2,1)}, bf16[2,320,768]{2,1,0:T(8,128)(2,1)}, u32[]{:S(2)}, u32[]{:S(2)}) collective-permute-start(bf16[2,320,768]{2,1,0:T(8,128)(2,1)} %get-tuple-element.73), channel_id=1, source_target_pairs={{1,0},{2,1},{3,2},{5,4},{6,5},{7,6},{9,8},{10,9},{11,10},{13,12},{... | collective-permute-start | bytes 2949128 | tf_op jit(solution)/shard_map/ppermute | solution.py:370
  263.4 106.3 %collective-permute-start.28 = (bf16[2,320,768]{2,1,0:T(8,128)(2,1)}, bf16[2,320,768]{2,1,0:T(8,128)(2,1)}, u32[]{:S(2)}, u32[]{:S(2)}) collective-permute-start(bf16[2,320,768]{2,1,0:T(8,128)(2,1)} %get-tuple-element.75), channel_id=1, source_target_pairs={{2,0},{3,1},{6,4},{7,5},{10,8},{11,9},{14,12},{15,13},{18,16},{19,... | collective-permute-start | bytes 2949128 | tf_op jit(solution)/shard_map/ppermute | solution.py:370
  264.7 173.2 %collective-permute-start.29 = (bf16[2,320,768]{2,1,0:T(8,128)(2,1)}, bf16[2,320,768]{2,1,0:T(8,128)(2,1)}, u32[]{:S(2)}, u32[]{:S(2)}) collective-permute-start(bf16[2,320,768]{2,1,0:T(8,128)(2,1)} %get-tuple-element.74), channel_id=1, source_target_pairs={{3,0},{7,4},{11,8},{15,12},{19,16},{23,20},{27,24},{31,28}} | collective-permute-start | bytes 2949128 | tf_op jit(solution)/shard_map/ppermute | solution.py:370
  266.2 23.6 %collective-permute-start.45 = (bf16[480,960]{1,0:T(8,128)(2,1)}, bf16[480,960]{1,0:T(8,128)(2,1)}, u32[]{:S(2)}, u32[]{:S(2)}) collective-permute-start(bf16[480,960]{1,0:T(8,128)(2,1)} %convolution_convert_fusion.8), channel_id=1, source_target_pairs={{0,4},{4,0},{8,12},{12,8},{16,20},{20,16},{24,28},{28,24},{1,5},{5... | collective-permute-start | bytes 2764808 | tf_op jit(solution)/shard_map/ppermute | solution.py:214
  266.8 205.9 %collective-permute-start.40 = (bf16[480,2560]{1,0:T(8,128)(2,1)}, bf16[480,2560]{1,0:T(8,128)(2,1)}, u32[]{:S(2)}, u32[]{:S(2)}) collective-permute-start(bf16[480,2560]{1,0:T(8,128)(2,1)} %convolution_convert_fusion), channel_id=1, source_target_pairs={{0,4},{4,0},{8,12},{12,8},{16,20},{20,16},{24,28},{28,24},{1,5},{5... | collective-permute-start | bytes 7372808 | tf_op jit(solution)/shard_map/ppermute | solution.py:214
  289.8 190.7 %collective-permute-start.35 = (bf16[480,2560]{1,0:T(8,128)(2,1)}, bf16[480,2560]{1,0:T(8,128)(2,1)}, u32[]{:S(2)}, u32[]{:S(2)}) collective-permute-start(bf16[480,2560]{1,0:T(8,128)(2,1)} %convolution_convert_fusion.2), channel_id=1, source_target_pairs={{0,4},{4,0},{8,12},{12,8},{16,20},{20,16},{24,28},{28,24},{1,5},{5... | collective-permute-start | bytes 7372808 | tf_op jit(solution)/shard_map/ppermute | solution.py:214
  339.9 147.8 %collective-permute-start.30 = (bf16[480,2560]{1,0:T(8,128)(2,1)}, bf16[480,2560]{1,0:T(8,128)(2,1)}, u32[]{:S(2)}, u32[]{:S(2)}) collective-permute-start(bf16[480,2560]{1,0:T(8,128)(2,1)} %convolution_convert_fusion.4), channel_id=1, source_target_pairs={{0,4},{4,0},{8,12},{12,8},{16,20},{20,16},{24,28},{28,24},{1,5},{5... | collective-permute-start | bytes 7372808 | tf_op jit(solution)/shard_map/ppermute | solution.py:214
  369.7 94.2 %collective-permute-start.46 = (bf16[2,120,384]{1,2,0:T(8,128)(2,1)}, bf16[2,120,384]{1,2,0:T(8,128)(2,1)}, u32[]{:S(2)}, u32[]{:S(2)}) collective-permute-start(bf16[2,120,384]{1,2,0:T(8,128)(2,1)} %pad_maximum_fusion.22), channel_id=1, source_target_pairs={{0,8},{4,12},{8,0},{12,4},{16,24},{20,28},{24,16},{28,20},{1,9},{5... | collective-permute-start | bytes 552968 | tf_op jit(solution)/shard_map/ppermute | solution.py:214
  437.9 27.0 %collective-permute-start.48 = (bf16[2,120,576]{1,2,0:T(8,128)(2,1)}, bf16[2,120,576]{1,2,0:T(8,128)(2,1)}, u32[]{:S(2)}, u32[]{:S(2)}) collective-permute-start(bf16[2,120,576]{1,2,0:T(8,128)(2,1)} %copy.79), channel_id=1, source_target_pairs={{0,16},{4,20},{8,24},{12,28},{16,0},{20,4},{24,8},{28,12},{1,17},{... | collective-permute-start | bytes 829448 | tf_op jit(solution)/shard_map/ppermute | solution.py:214
  463.9 31.1 %collective-permute-start.50 = (bf16[480,1602]{1,0:T(8,128)(2,1)S(1)}, bf16[480,1602]{1,0:T(8,128)(2,1)S(1)}, u32[]{:S(2)}, u32[]{:S(2)}) collective-permute-start(bf16[480,1602]{1,0:T(8,128)(2,1)S(1)} %concatenate.78), channel_id=1, source_target_pairs={{0,4},{4,0},{8,12},{12,8},{16,20},{20,16},{24,28},{28,24},{1,5},{5... | collective-permute-start | bytes 4613768 | tf_op jit(solution)/shard_map/ppermute | solution.py:214
  470.2 80.1 %collective-permute-start.49 = (bf16[120,576]{0,1:T(8,128)(2,1)}, bf16[120,576]{0,1:T(8,128)(2,1)}, u32[]{:S(2)}, u32[]{:S(2)}) collective-permute-start(bf16[120,576]{0,1:T(8,128)(2,1)} %fusion.101), channel_id=1, source_target_pairs={{0,8},{4,12},{8,0},{12,4},{16,24},{20,28},{24,16},{28,20},{1,9},{5... | collective-permute-start | bytes 414728 | tf_op jit(solution)/shard_map/ppermute | solution.py:214
  487.7 22.5 %collective-permute-start.36 = (bf16[2,120,1280]{2,1,0:T(8,128)(2,1)}, bf16[2,120,1280]{2,1,0:T(8,128)(2,1)}, u32[]{:S(2)}, u32[]{:S(2)}) collective-permute-start(bf16[2,120,1280]{2,1,0:T(8,128)(2,1)} %pad_maximum_fusion.12), channel_id=1, source_target_pairs={{0,8},{4,12},{8,0},{12,4},{16,24},{20,28},{24,16},{28,20},{1,9},{5... | collective-permute-start | bytes 1843208 | tf_op jit(solution)/shard_map/ppermute | solution.py:214
  497.0 26.2 %collective-permute-start.31 = (bf16[2,120,1280]{2,1,0:T(8,128)(2,1)}, bf16[2,120,1280]{2,1,0:T(8,128)(2,1)S(1)}, u32[]{:S(2)}, u32[]{:S(2)}) collective-permute-start(bf16[2,120,1280]{2,1,0:T(8,128)(2,1)} %pad_maximum_fusion.10), channel_id=1, source_target_pairs={{0,8},{4,12},{8,0},{12,4},{16,24},{20,28},{24,16},{28,20},{1,9},{5... | collective-permute-start | bytes 1843208 | tf_op jit(solution)/shard_map/ppermute | solution.py:214
  497.6 27.6 %collective-permute-start.33 = (bf16[2,120,1280]{2,1,0:T(8,128)(2,1)}, bf16[2,120,1280]{2,1,0:T(8,128)(2,1)S(1)}, u32[]{:S(2)}, u32[]{:S(2)}) collective-permute-start(bf16[2,120,1280]{2,1,0:T(8,128)(2,1)} %slice.529), channel_id=1, source_target_pairs={{0,16},{4,20},{8,24},{12,28},{16,0},{20,4},{24,8},{28,12},{1,17},{... | collective-permute-start | bytes 1843208 | tf_op jit(solution)/shard_map/ppermute | solution.py:214
  510.2 35.1 %collective-permute-start.42 = (bf16[120,1280]{1,0:T(8,128)(2,1)S(1)}, bf16[120,1280]{1,0:T(8,128)(2,1)S(1)}, u32[]{:S(2)}, u32[]{:S(2)}) collective-permute-start(bf16[120,1280]{1,0:T(8,128)(2,1)S(1)} %get-tuple-element.82), channel_id=1, source_target_pairs={{0,16},{4,20},{8,24},{12,28},{16,0},{20,4},{24,8},{28,12},{1,17},{... | collective-permute-start | bytes 921608 | tf_op jit(solution)/shard_map/ppermute | solution.py:214
  512.1 33.2 %collective-permute-start.44 = (bf16[120,1280]{1,0:T(8,128)(2,1)S(1)}, bf16[120,1280]{1,0:T(8,128)(2,1)S(1)}, u32[]{:S(2)}, u32[]{:S(2)}) collective-permute-start(bf16[120,1280]{1,0:T(8,128)(2,1)S(1)} %get-tuple-element.83), channel_id=1, source_target_pairs={{0,8},{4,12},{8,0},{12,4},{16,24},{20,28},{24,16},{28,20},{1,9},{5... | collective-permute-start | bytes 921608 | tf_op jit(solution)/shard_map/ppermute | solution.py:214
  547.7 121.9 %all-reduce.5.cloned.1.call-start = ((), (), s32[]{:S(2)}) async-start(), calls=%async_computation | async-start | bytes 1314816 | tf_op jit(solution)/shard_map/psum | solution.py:387
  (83 other events, 1104.2 us)
Sparse Core Ops, SparseCore 0:
  547.8 76.6 all-reduce.6
  629.2 40.3 all-reduce.4

commit v3 on v2

--- a/solution.py
+++ b/solution.py
@@ -29,10 +29,9 @@
 
 
 def fill_bias(info_ref, bias, tok):
-    pack = pl.program_id(0)
-    own = info_ref[pack, 0]
-    first_end = info_ref[pack, 1]
-    second_end = info_ref[pack, 2]
+    own = info_ref[0, 0]
+    first_end = info_ref[0, 1]
+    second_end = info_ref[0, 2]
     query = own * tok + lax.broadcasted_iota(jnp.int32, (tok, tok), 1)
     start = jnp.where(
         query >= second_end, second_end, jnp.where(query >= first_end, first_end, 0)
@@ -48,9 +47,9 @@
 
 
 def forward_kernel(tok, info_ref, q_ref, kv_ref, attn_ref, lse_ref, bias):
-    own = info_ref[pl.program_id(0), 0]
-
-    @pl.when(pl.program_id(1) == 0)
+    own = info_ref[0, 0]
+
+    @pl.when(pl.program_id(0) == 0)
     def _():
         fill_bias(info_ref, bias, tok)
 
@@ -88,9 +87,9 @@
 def backward_kernel(
     tok, count, info_ref, q_ref, kv_ref, do_ref, attn_ref, lse_ref, dq_ref, dkv_ref, bias
 ):
-    own = info_ref[pl.program_id(0), 0]
-
-    @pl.when(pl.program_id(1) == 0)
+    own = info_ref[0, 0]
+
+    @pl.when(pl.program_id(0) == 0)
     def _():
         fill_bias(info_ref, bias, tok)
 
@@ -135,58 +134,67 @@
     lax.fori_loop(own + 1, count, blank, 0)
 
 
-def attention_specs(tok, count):
+def attention_specs(pack, tok, count):
     return (
         pl.BlockSpec(memory_space=pltpu.SMEM),
-        pl.BlockSpec((GROUPS * HD, tok), lambda b, k: (k, b)),
-        pl.BlockSpec((count, 2, HD, tok), lambda b, k: (0, 0, k, b)),
-        pl.BlockSpec((1, GROUPS, tok), lambda b, k: (k, 0, b)),
+        pl.BlockSpec((GROUPS * HD, tok), lambda k: (k, pack)),
+        pl.BlockSpec((GROUPS * HD, tok), lambda k: (k, 0)),
+        pl.BlockSpec((count, 2, HD, tok), lambda k: (0, 0, k, 0)),
+        pl.BlockSpec((1, GROUPS, tok), lambda k: (k, 0, 0)),
     )
 
 
 PARAMS = dict(vmem_limit_bytes=48 * 1024 * 1024)
 
 
-def attend_forward(info, queries, kv, packs, tok, count):
-    smem, rows, pairs, stats = attention_specs(tok, count)
-    pairs_done = packs * H * tok * tok * count
+def with_awaited(kernel, operands, awaited):
+    def body(*refs):
+        kernel(*refs[:operands], *refs[operands + awaited :])
+
+    return body
+
+
+def attend_forward(pack, info, queries, kv, awaited, tok, count):
+    smem, columns, rows, pairs, stats = attention_specs(pack, tok, count)
+    pairs_done = H * tok * tok * count
     return pl.pallas_call(
-        functools.partial(forward_kernel, tok),
-        grid=(packs, KVH),
-        in_specs=[smem, rows, pairs],
+        with_awaited(functools.partial(forward_kernel, tok), 3, len(awaited)),
+        grid=(KVH,),
+        in_specs=[smem, columns, pairs] + [pl.BlockSpec(memory_space=pl.ANY)] * len(awaited),
         out_specs=[rows, stats],
         out_shape=[
-            jax.ShapeDtypeStruct((QW, packs * tok), BF16),
-            jax.ShapeDtypeStruct((KVH, GROUPS, packs * tok), F32),
+            jax.ShapeDtypeStruct((QW, tok), BF16),
+            jax.ShapeDtypeStruct((KVH, GROUPS, tok), F32),
         ],
         scratch_shapes=[pltpu.VMEM((count, tok, tok), F32)],
         compiler_params=pltpu.CompilerParams(**PARAMS),
         cost_estimate=pl.CostEstimate(
-            flops=16 * HD * pairs_done, bytes_accessed=10_000_000, transcendentals=pairs_done
+            flops=16 * HD * pairs_done, bytes_accessed=5_000_000, transcendentals=pairs_done
         ),
         name="attend_forward",
-    )(info, queries, kv)
-
-
-def attend_backward(info, queries, kv, d_attn, attn, lse, packs, tok, count):
-    smem, rows, pairs, stats = attention_specs(tok, count)
-    pairs_done = packs * H * tok * tok * count
+    )(info, queries, kv, *awaited)
+
+
+def attend_backward(pack, info, queries, kv, d_attn, attn, lse, awaited, tok, count):
+    smem, columns, rows, pairs, stats = attention_specs(pack, tok, count)
+    pairs_done = H * tok * tok * count
     return pl.pallas_call(
-        functools.partial(backward_kernel, tok, count),
-        grid=(packs, KVH),
-        in_specs=[smem, rows, pairs, rows, rows, stats],
+        with_awaited(functools.partial(backward_kernel, tok, count), 6, len(awaited)),
+        grid=(KVH,),
+        in_specs=[smem, columns, pairs, columns, rows, stats]
+        + [pl.BlockSpec(memory_space=pl.ANY)] * len(awaited),
         out_specs=[rows, pairs],
         out_shape=[
-            jax.ShapeDtypeStruct((QW, packs * tok), F32),
-            jax.ShapeDtypeStruct((count, 2, KW, packs * tok), BF16),
+            jax.ShapeDtypeStruct((QW, tok), F32),
+            jax.ShapeDtypeStruct((count, 2, KW, tok), BF16),
         ],
         scratch_shapes=[pltpu.VMEM((count, tok, tok), F32)],
         compiler_params=pltpu.CompilerParams(**PARAMS),
         cost_estimate=pl.CostEstimate(
-            flops=40 * HD * pairs_done, bytes_accessed=20_000_000, transcendentals=pairs_done
+            flops=40 * HD * pairs_done, bytes_accessed=10_000_000, transcendentals=pairs_done
         ),
         name="attend_backward",
-    )(info, queries, kv, d_attn, attn, lse)
+    )(info, queries, kv, d_attn, attn, lse, *awaited)
 
 
 def rotate(values, cosine, sine):
@@ -214,9 +222,12 @@
     return lax.ppermute(value, "dp", [(i, i ^ bit) for i in range(8)])
 
 
-def gather_shards(shard):
+def gather_near(shard):
+    return shard, swap(shard, 2), swap(shard, 4)
+
+
+def gather_rest(shard, from_x, from_y):
     middle = shard.shape[0] // 16 * 8
-    from_x, from_y = swap(shard, 2), swap(shard, 4)
     diagonal = jnp.concatenate([swap(from_x[:middle], 4), swap(from_y[middle:], 2)], 0)
     near = (shard, from_x, from_y, diagonal)
     return jnp.concatenate(near + tuple(swap(part, 1) for part in near), 0)
@@ -226,10 +237,12 @@
     return (left.astype(F32) + right.astype(F32)).astype(BF16)
 
 
-def reduce_shards(keep, send):
-    columns = keep.shape[1]
-    own = add(keep, swap(send, 1)).reshape(4, -1, columns)
-    split = columns // 256 * 128
+def reduce_cores(keep, send):
+    return add(keep, swap(send, 1)).reshape(4, -1, keep.shape[1])
+
+
+def reduce_chips(own):
+    split = own.shape[2] // 256 * 128
     one = own[:, :, :split]
     two = own[:, :, split:]
     from_x = swap(jnp.stack([one[1], one[3]]), 2)
@@ -239,6 +252,17 @@
     done_one = add(add(one[0], from_x[0]), last_y)
     done_two = add(add(two[0], from_y[0]), last_x)
     return jnp.concatenate([done_one, done_two], 1)
+
+
+def sum_over_ctx(value, count):
+    if count & (count - 1):
+        return lax.psum(value, "ctx")
+    step = 1
+    while step < count:
+        moved = lax.ppermute(value, "ctx", [(i, i ^ step) for i in range(count)])
+        value = add(value, moved)
+        step *= 2
+    return value
 
 
 def local(
@@ -276,19 +300,26 @@
     def restore(value):
         return dot(value, chosen, ((1,), (1,))).astype(BF16) if direct else value
 
-    def gathered(value):
+    def gather_begin(value):
+        return gather_near(value) if direct else (value,)
+
+    def gather_end(parts):
         if direct:
-            return gather_shards(value)
-        return lax.all_gather(value, "dp", axis=0, tiled=True)
-
-    full_qkv = gathered(
-        jnp.concatenate([w_query, w_key, w_value, gain_attn[:, None], gain_ffn[:, None]], 1)
+            return gather_rest(*parts)
+        return lax.all_gather(parts[0], "dp", axis=0, tiled=True)
+
+    full_qkv = gather_end(
+        gather_begin(
+            jnp.concatenate([w_query, w_key, w_value, gain_attn[:, None], gain_ffn[:, None]], 1)
+        )
     )
     down_out = jnp.concatenate([w_down.T, w_out.T], 1)
     gate_up = jnp.concatenate([w_gate, w_up], 1)
     full_qkv, down_out, gate_up = lax.optimization_barrier((full_qkv, down_out, gate_up))
-    full_gate_up = gathered(gate_up)
-    full_down_out = gathered(down_out)
+    near_down_out = gather_begin(down_out)
+    near_gate_up = gather_begin(gate_up)
+    full_down_out = gather_end(near_down_out)
+    full_gate_up = gather_end(near_gate_up)
     full_down_t, full_out_t = full_down_out[:, :FF], full_down_out[:, FF:]
     gains = full_qkv[:, QW + 2 * KW :].astype(F32).T
     gain_one, gain_two = gains[0], gains[1]
@@ -315,15 +346,26 @@
     keys = rotate(qkv[QW : QW + KW], cosine, sine).astype(BF16)
     values = qkv[QW + KW : QW + 2 * KW].astype(BF16)
     own_kv = jnp.stack([keys, values])
-    kv = jnp.stack(
-        [own_kv]
-        + [
-            lax.ppermute(own_kv, "ctx", [(i, i + d) for i in range(count - d)])
-            for d in range(1, count)
-        ]
-    )
-
-    attn, lse = attend_forward(info, queries, kv, packs, tok, count)
+
+    def spread(block):
+        return jnp.stack(
+            [block]
+            + [
+                lax.ppermute(block, "ctx", [(i, i + d) for i in range(count - d)])
+                for d in range(1, count)
+            ]
+        )
+
+    kv = [spread(own_kv[:, :, b * tok : (b + 1) * tok]) for b in range(packs)]
+    attn_parts, lse = [], []
+    for b in range(packs):
+        awaited = near_down_out[1:] + near_gate_up[1:] if b == packs - 1 else ()
+        attn_part, lse_part = attend_forward(
+            b, info[b : b + 1], queries, kv[b], awaited, tok, count
+        )
+        attn_parts.append(attn_part)
+        lse.append(lse_part)
+    attn = jnp.concatenate(attn_parts, 1)
 
     middle = stream + dot(attn, full_out_t, ((0,), (1,)))
     inverse_two = lax.rsqrt(jnp.mean(middle * middle, -1, keepdims=True) + NORM_EPSILON)
@@ -338,20 +380,27 @@
     d_gate = (d_hidden * up * sigma * (1.0 + gate * (1.0 - sigma))).astype(BF16)
     d_up = (d_hidden * silu).astype(BF16)
 
-    def reduced(left, right, axis, extra=()):
+    def reduce_begin(left, right, axis, extra=()):
         def term(part, extra_part):
             product = dot(part, right, ((0,), (axis,))).astype(BF16)
             return jnp.concatenate((product,) + extra_part, 1)
 
         if not direct:
-            return lax.psum_scatter(term(left, extra), "dp", scatter_dimension=0, tiled=True)
+            return term(left, extra)
         send = term(left[:, half_model:], tuple(e[half_model:] for e in extra))
         keep = term(left[:, :half_model], tuple(e[:half_model] for e in extra))
-        return reduce_shards(keep, send)
-
-    p_down = reduced(cot, hidden, 0)
-    p_gate = reduced(normed_two, d_gate, 0)
-    p_up = reduced(normed_two, d_up, 0)
+        return reduce_cores(keep, send)
+
+    def reduce_end(value):
+        if direct:
+            return reduce_chips(value)
+        return lax.psum_scatter(value, "dp", scatter_dimension=0, tiled=True)
+
+    begun = [
+        reduce_begin(cot, hidden, 0),
+        reduce_begin(normed_two, d_gate, 0),
+        reduce_begin(normed_two, d_up, 0),
+    ]
 
     output = (middle + dot(hidden, full_down_t, ((1,), (1,)))).astype(BF16)
 
@@ -363,12 +412,22 @@
     d_mixed = d_middle.astype(BF16)
     d_attn = dot(full_out_t, d_mixed, ((0,), (1,))).astype(BF16)
 
-    dq, dkv_terms = attend_backward(info, queries, kv, d_attn, attn, lse, packs, tok, count)
-    p_out = reduced(d_mixed, attn, 1)
-    dkv = dkv_terms[0].astype(F32)
-    for d in range(1, count):
-        moved = lax.ppermute(dkv_terms[d], "ctx", [(i + d, i) for i in range(count - d)])
-        dkv = dkv + moved.astype(F32)
+    begun.append(reduce_begin(d_mixed, attn, 1))
+    dq_parts, dkv_parts = [], []
+    for b in range(packs):
+        awaited = tuple(begun) if b == packs - 1 else ()
+        dq_part, terms = attend_backward(
+            b, info[b : b + 1], queries, kv[b], d_attn, attn_parts[b], lse[b], awaited, tok, count
+        )
+        dkv_part = terms[0].astype(F32)
+        for d in range(1, count):
+            moved = lax.ppermute(terms[d], "ctx", [(i + d, i) for i in range(count - d)])
+            dkv_part = dkv_part + moved.astype(F32)
+        dq_parts.append(dq_part)
+        dkv_parts.append(dkv_part)
+    dq = jnp.concatenate(dq_parts, 1)
+    dkv = jnp.concatenate(dkv_parts, 2)
+    early = lax.psum(tuple(reduce_end(value) for value in begun), "ctx")
 
     d_query = rotate(dq * (1 / math.sqrt(HD)), cosine, -sine).astype(BF16)
     d_key = rotate(dkv[0], cosine, -sine).astype(BF16)
@@ -377,16 +436,15 @@
         jnp.concatenate([d_qkv, jnp.zeros((2, rows), BF16)], 0), full_qkv, ((0,), (1,))
     )
     d_gain_one, d_stream = norm_back(d_normed, stream, inverse_one, gain_one)
-    p_qkv = reduced(
-        normed, d_qkv, 1, (d_gain_one.astype(BF16)[:, None], d_gain_two.astype(BF16)[:, None])
+    p_qkv = reduce_end(
+        reduce_begin(
+            normed, d_qkv, 1, (d_gain_one.astype(BF16)[:, None], d_gain_two.astype(BF16)[:, None])
+        )
     )
     d_tokens = restore((d_middle + d_stream).astype(BF16))
 
-    early = lax.psum((p_down, p_gate, p_up), "ctx")
-    early, p_out, p_qkv = lax.optimization_barrier((early, p_out, p_qkv))
-    late = lax.psum((p_out, p_qkv), "ctx")
-    g_down, g_gate, g_up = (value.astype(F32) for value in early)
-    g_out, g_qkv = (value.astype(F32) for value in late)
+    g_down, g_gate, g_up, g_out = (value.astype(F32) for value in early)
+    g_qkv = sum_over_ctx(p_qkv, count).astype(F32)
 
     return (
         restore(output).reshape(packs, tok, D),

time: 688 us -> 664 us (0.965)
  waiting for transfers between devices: 355 us -> 259 us
  starting transfers between devices: 52.1 us -> 110 us
  local copies, waits for them, and re-layouts: 61.2 us -> 76.9 us
    ppermute x6 -> x14, starting transfers between devices: 13.7 us -> 73.1 us  [the longest x6 64.7 us: spread(): lax.ppermute(block, 'ctx', [(i, i + d) for i in range(count - d)])]
    psum x2 -> x1, waiting for transfers between devices: 93 us -> 43.5 us  [local(): early = lax.psum(tuple((reduce_end(value) for value in begun)), 'ctx')]
    ppermute x6 -> x14, waiting for transfers between devices: 188 us -> 144 us  [the longest x6 129 us: local(): lax.ppermute(terms[d], 'ctx', [(i + d, i) for i in range(count - d)])]
    unnamed x159 -> x166, local copies, waits for them, and re-layouts: 37.9 us -> 49 us
    convert_element_type x15 -> x17, other arithmetic: 13.4 us -> 16 us  [add(): return (left.astype(F32) + right.astype(F32)).astype(BF16)]
    pallas_call x2 -> x4, Pallas kernels: 33.4 us -> 35.3 us  [the longest x2 19.5 us: attend_backward(): pl.pallas_call(with_awaited(functools.partial(backward_kernel, tok, count...]
  transfers between devices with their start and end apart: 57 -> 64, of which waited for: 28 -> 22; matrix products, arithmetic and copies ran while one was open for 18% -> 20% of each run, Pallas kernels for 2% -> 5%
where the time goes in v3:
time: 664 us; the launch traced here: 659 us
  waiting for transfers between devices  259 us (39%)
  matrix products  119 us (18%)
  starting transfers between devices  110 us (17%)
  local copies, waits for them, and re-layouts  76.9 us (12%)
  other arithmetic  42.9 us (6%)
  Pallas kernels  35.3 us (5%)
  between operations  15.7 us (2%)
    ppermute x6, waiting for transfers between devices, local(): lax.ppermute(terms[d], 'ctx', [(i + d, i) for i in range(count - d)])  129 us
    dot_general x22, matrix products, dot(): lax.dot_general(left, right, (dims, ((), ())), preferred_element_type=F32)  119 us
    ppermute x49, waiting for transfers between devices, swap(): return lax.ppermute(value, 'dp', [(i, i ^ bit) for i in range(8)])  70.8 us
    ppermute x6, starting transfers between devices, spread(): lax.ppermute(block, 'ctx', [(i, i + d) for i in range(count - d)])  64.7 us
    unnamed x166, local copies, waits for them, and re-layouts  49 us
    psum x1, waiting for transfers between devices, local(): early = lax.psum(tuple((reduce_end(value) for value in begun)), 'ctx')  43.5 us
    ppermute x49, starting transfers between devices, swap(): return lax.ppermute(value, 'dp', [(i, i ^ bit) for i in range(8)])  37.2 us
    pallas_call x2, Pallas kernels, attend_backward(): pl.pallas_call(with_awaited(functools.partial(backward_kernel, tok, count...  19.5 us
  transfers between devices with their start and end apart: 64, of which 22 were waited for; matrix products, arithmetic and copies ran while one was open for 20% of the time, Pallas kernels for 5%

profile of v3, /device:TPU:0, one launch (start us, length us, event | category | flops | bytes accessed | tf_op | source)
XLA Modules:
  0.0 659.2 jit_solution(17376309731226639099)
XLA Ops:
  54.1 4.5 collective-permute-start.9
  65.7 24.1 %collective-permute-start.11 = (bf16[2,320,384]{2,1,0:T(8,128)(2,1)S(1)}, bf16[2,320,384]{2,1,0:T(8,128)(2,1)S(1)}, u32[]{:S(2)}, u32[]{:S(2)}) collective-permute-start(bf16[2,320,384]{2,1,0:T(8,128)(2,1)S(1)} %get-tuple-element.110), channel_id=1, source_target_pairs={{0,1},{1,2},{2,3},{4,5},{5,6},{6,7},{8,9},{9,10},{10,11},{12,13},{... | collective-permute-start | bytes 1474568 | tf_op jit(solution)/shard_map/ppermute | solution.py:354
  89.9 4.3 collective-permute-start.12
  94.2 26.6 %collective-permute-start.13 = (bf16[2,320,384]{2,1,0:T(8,128)(2,1)S(1)}, bf16[2,320,384]{2,1,0:T(8,128)(2,1)S(1)}, u32[]{:S(2)}, u32[]{:S(2)}) collective-permute-start(bf16[2,320,384]{2,1,0:T(8,128)(2,1)S(1)} %get-tuple-element.110), channel_id=1, source_target_pairs={{0,3},{4,7},{8,11},{12,15},{16,19},{20,23},{24,27},{28,31}} | collective-permute-start | bytes 1474568 | tf_op jit(solution)/shard_map/ppermute | solution.py:354
  121.1 7.7 %attend_forward.2 = (bf16[960,384]{1,0:T(8,128)(2,1)S(1)}, f32[5,3,384]{2,1,0:T(4,128)S(1)}) custom-call(s32[1,4]{1,0:T(1,128)S(1)} %get-tuple-element.128.refs_0_, bf16[960,768]{1,0:T(8,128)(2,1)S(1)} %bitcast.203, bf16[4,2,320,384]{3,2,1,0:T(8,128)(2,1)S(1)} %pad_maximum_fusion.1.refs_2_), custom_call_target="tpu_custom_call" | custom-call | flops 9059696640 | bytes 5000000 | tf_op jit(solution)/shard_map/attend_forward/pallas_call | solution.py:160
  136.8 13.7 %collective-permute-done.16.refs_5_ = bf16[120,5120]{1,0:T(8,128)(2,1)S(1)} collective-permute-done((bf16[120,5120]{1,0:T(8,128)(2,1)S(1)}, bf16[120,5120]{1,0:T(8,128)(2,1)S(1)}, u32[]{:S(2)}, u32[]{:S(2)}) %collective-permute-start.16) | collective-permute-done | bytes 1228832 | tf_op jit(solution)/shard_map/ppermute | solution.py:222
  152.1 8.1 %attend_forward.3 = (bf16[960,384]{1,0:T(8,128)(2,1)S(1)}, f32[5,3,384]{2,1,0:T(4,128)S(1)}) custom-call(s32[1,4]{1,0:T(1,128)S(1)} %get-tuple-element.127.refs_0_, bf16[960,768]{1,0:T(8,128)(2,1)} %bitcast.204, bf16[4,2,320,384]{3,2,1,0:T(8,128)(2,1)} %pad_maximum_fusion.2.refs_2_, bf16[120,3520]{1,0:T(8,128)(2,1)S(1)} %collective-permute-done.14.refs_3_, ...), custom_call_target="tpu_custom_call" | custom-call | flops 9059696640 | bytes 5000000 | tf_op jit(solution)/shard_map/attend_forward/pallas_call | solution.py:160
  166.8 13.3 %collective-permute-done.24 = bf16[56,5120]{1,0:T(8,128)(2,1)S(1)} collective-permute-done((bf16[56,5120]{1,0:T(8,128)(2,1)S(1)}, bf16[56,5120]{1,0:T(8,128)(2,1)S(1)}, u32[]{:S(2)}, u32[]{:S(2)}) %collective-permute-start.24) | collective-permute-done | bytes 573472 | tf_op jit(solution)/shard_map/ppermute | solution.py:222
  195.5 11.1 %fusion.133 = f32[768,5120]{1,0:T(8,128)} fusion(bf16[768,960]{0,1:T(8,128)(2,1)S(1)} %multiply_convert_fusion.3, bf16[960,5120]{1,0:T(8,128)(2,1)S(1)} %constant_dynamic-update-slice_fusion.20), kind=kOutput, calls=%fused_computation.286 | convolution fusion | flops 7549747200 | bytes 27033600 | tf_op jit(solution)/shard_map/dot_general | solution.py:28
  206.6 25.6 %multiply_convert_fusion.1 = (bf16[768,2560]{1,0:T(8,128)(2,1)}, bf16[768,2560]{1,0:T(8,128)(2,1)}, bf16[768,2560]{1,0:T(8,128)(2,1)}) fusion(f32[768,5120]{1,0:T(8,128)} %fusion.133, bf16[960,768]{1,0:T(8,128)(2,1)S(1)} %copy-done.18, bf16[960,3520]{1,0:T(8,128)(2,1)} %copy-done.47), kind=kOutput, calls=%fused_computation.1 | convolution fusion | flops 3804364800 | bytes 33914880 | tf_op jit(solution)/shard_map/dot_general | solution.py:28
  232.2 5.8 convolution_convert_fusion
  238.1 7.7 %fusion.1 = f32[768,960]{0,1:T(8,128)} fusion(bf16[768,2560]{1,0:T(8,128)(2,1)} %get-tuple-element.68, bf16[960,5120]{1,0:T(8,128)(2,1)S(1)} %copy-done.42), kind=kOutput, calls=%fused_computation.5 | convolution fusion | flops 3774873600 | bytes 11796480 | tf_op jit(solution)/shard_map/dot_general | solution.py:28
  245.8 7.4 %multiply_reduce_fusion = (bf16[960]{0:T(1024)(128)(2,1)S(1)}, f32[768]{0:T(1024)S(1)}, f32[768,960]{0,1:T(8,128)S(1)}) fusion(f32[768,960]{0,1:T(8,128)S(1)} %get-tuple-element.134, f32[768]{0:T(1024)S(1)} %get-tuple-element.122, f32[960]{0:T(1024)S(1)} %get-tuple-element.59, f32[768,960]{0,1:T(8,128)} %fusion.1, bf16[768,2560]{1,0:T(8,128)(2,1)} %get-tuple-element.67, ...), kind=kOutput, calls=%fused_computation.45 | convolution fusion | flops 3780032768 | bytes 17707904 | tf_op jit(solution)/shard_map/dot_general | solution.py:28
  265.6 9.9 %attend_backward.2 = (f32[960,384]{1,0:T(8,128)S(1)}, bf16[4,2,320,384]{3,2,1,0:T(8,128)(2,1)}) custom-call(s32[1,4]{1,0:T(1,128)S(1)} %get-tuple-element.128.refs_0_, bf16[960,768]{1,0:T(8,128)(2,1)S(1)} %bitcast.205, bf16[4,2,320,384]{3,2,1,0:T(8,128)(2,1)} %copy-done, bf16[960,768]{1,0:T(8,128)(2,1)S(1)} %fusion.49.refs_3_, ...), custom_call_target="tpu_custom_call" | custom-call | flops 22649241600 | bytes 10000000 | tf_op jit(solution)/shard_map/attend_backward/pallas_call | solution.py:181
  285.2 36.4 %collective-permute-done.34 = bf16[2,320,384]{2,1,0:T(8,128)(2,1)S(1)} collective-permute-done((bf16[2,320,384]{2,1,0:T(8,128)(2,1)S(1)}, bf16[2,320,384]{2,1,0:T(8,128)(2,1)S(1)}, u32[]{:S(2)}, u32[]{:S(2)}) %collective-permute-start.34) | collective-permute-done | bytes 491552 | tf_op jit(solution)/shard_map/ppermute | solution.py:424
  321.6 14.1 %collective-permute-done.35 = bf16[2,320,384]{2,1,0:T(8,128)(2,1)S(1)} collective-permute-done((bf16[2,320,384]{2,1,0:T(8,128)(2,1)S(1)}, bf16[2,320,384]{2,1,0:T(8,128)(2,1)S(1)}, u32[]{:S(2)}, u32[]{:S(2)}) %collective-permute-start.35) | collective-permute-done | bytes 491552 | tf_op jit(solution)/shard_map/ppermute | solution.py:424
  336.2 37.4 %collective-permute-done.36 = bf16[2,320,384]{2,1,0:T(8,128)(2,1)S(1)} collective-permute-done((bf16[2,320,384]{2,1,0:T(8,128)(2,1)S(1)}, bf16[2,320,384]{2,1,0:T(8,128)(2,1)S(1)}, u32[]{:S(2)}, u32[]{:S(2)}) %collective-permute-start.36) | collective-permute-done | bytes 491552 | tf_op jit(solution)/shard_map/ppermute | solution.py:424
  377.0 6.3 collective-permute-done.49
  389.4 3.9 add_convert_fusion.2
  394.2 3.9 add_convert_fusion
  407.7 9.6 %attend_backward.3 = (f32[960,384]{1,0:T(8,128)S(1)}, bf16[4,2,320,384]{3,2,1,0:T(8,128)(2,1)}) custom-call(s32[1,4]{1,0:T(1,128)S(1)} %get-tuple-element.127.refs_0_, bf16[960,768]{1,0:T(8,128)(2,1)S(1)} %bitcast.206, bf16[4,2,320,384]{3,2,1,0:T(8,128)(2,1)} %pad_maximum_fusion.2.refs_2_, bf16[960,768]{1,0:T(8,128)(2,1)S(1)} %fusion.49.refs_3_, ...), custom_call_target="tpu_custom_call" | custom-call | flops 22649241600 | bytes 10000000 | tf_op jit(solution)/shard_map/attend_backward/pallas_call | solution.py:181
  426.8 13.5 %collective-permute-done.37 = bf16[2,320,384]{2,1,0:T(8,128)(2,1)S(1)} collective-permute-done((bf16[2,320,384]{2,1,0:T(8,128)(2,1)S(1)}, bf16[2,320,384]{2,1,0:T(8,128)(2,1)S(1)}, u32[]{:S(2)}, u32[]{:S(2)}) %collective-permute-start.37) | collective-permute-done | bytes 491552 | tf_op jit(solution)/shard_map/ppermute | solution.py:424
  441.3 27.7 %collective-permute-done.39 = bf16[2,320,384]{2,1,0:T(8,128)(2,1)S(1)} collective-permute-done((bf16[2,320,384]{2,1,0:T(8,128)(2,1)S(1)}, bf16[2,320,384]{2,1,0:T(8,128)(2,1)S(1)}, u32[]{:S(2)}, u32[]{:S(2)}) %collective-permute-start.39) | collective-permute-done | bytes 491552 | tf_op jit(solution)/shard_map/ppermute | solution.py:424
  475.1 5.1 fusion.22
  487.0 3.9 concatenate.93
  498.1 9.6 %collective-permute-done.53 = bf16[2,120,1280]{2,1,0:T(8,128)(2,1)S(1)} collective-permute-done((bf16[2,120,1280]{2,1,0:T(8,128)(2,1)}, bf16[2,120,1280]{2,1,0:T(8,128)(2,1)S(1)}, u32[]{:S(2)}, u32[]{:S(2)}) %collective-permute-start.53) | collective-permute-done | bytes 614432 | tf_op jit(solution)/shard_map/ppermute | solution.py:222
  510.3 7.8 %collective-permute-done.56 = bf16[120,1280]{1,0:T(8,128)(2,1)S(1)} collective-permute-done((bf16[120,1280]{1,0:T(8,128)(2,1)S(1)}, bf16[120,1280]{1,0:T(8,128)(2,1)S(1)}, u32[]{:S(2)}, u32[]{:S(2)}) %collective-permute-start.56) | collective-permute-done | bytes 307232 | tf_op jit(solution)/shard_map/ppermute | solution.py:222
  521.1 3.8 collective-permute-done.52
  562.9 12.7 %fusion.46 = bf16[768,960]{0,1:T(8,128)(2,1)} fusion(s32[960]{0:T(1024)S(1)} %copy-done.55, f32[768,960]{0,1:T(8,128)S(1)} %get-tuple-element.134, bf16[768,2560]{1,0:T(8,128)(2,1)} %get-tuple-element.69, bf16[960,3520]{1,0:T(8,128)(2,1)} %copy-done.47), kind=kOutput, calls=%fused_computation.76 | convolution fusion | flops 5193584640 | bytes 13274880 | tf_op jit(solution)/shard_map/dot_general | solution.py:28
  575.6 12.6 %collective-permute-done.45 = bf16[120,1602]{0,1:T(8,128)(2,1)} collective-permute-done((bf16[120,1602]{0,1:T(8,128)(2,1)}, bf16[120,1602]{0,1:T(8,128)(2,1)}, u32[]{:S(2)}, u32[]{:S(2)}) %collective-permute-start.45) | collective-permute-done | bytes 384512 | tf_op jit(solution)/shard_map/ppermute | solution.py:262
  590.1 6.6 fusion.48
  598.6 43.5 %all-reduce.3.cloned.1.call-done = (bf16[960,120]{0,1:T(8,128)(2,1)}, bf16[120,2560]{1,0:T(8,128)(2,1)}, bf16[120,2560]{1,0:T(8,128)(2,1)}, bf16[2560,120]{0,1:T(8,128)(2,1)}) async-done(((bf16[960,120]{0,1:T(8,128)(2,1)}, bf16[120,2560]{1,0:T(8,128)(2,1)}, bf16[120,2560]{1,0:T(8,128)(2,1)}, bf16[2560,120]{0,1:T(8,128)(2,1)}), (bf16[960,120]{0,1:T(8,128)(2,1)}, bf16[120,2560]{1,0:T(8,128)(2,1)}, ...) | async-done | bytes 2073616 | tf_op jit(solution)/shard_map/psum | solution.py:430
  (414 shorter events, 215.4 us)
Async XLA Ops:
  7.2 635.0 %all-reduce.3.cloned.1.call-start = ((), (), s32[]{:S(2)}) async-start(), calls=%async_computation | async-start | bytes 4177920 | tf_op jit(solution)/shard_map/psum | solution.py:430
  16.5 23.6 %collective-permute-start.4 = (bf16[120,1602]{1,0:T(8,128)(2,1)S(1)}, bf16[120,1602]{1,0:T(8,128)(2,1)}, u32[]{:S(2)}, u32[]{:S(2)}) collective-permute-start(bf16[120,1602]{1,0:T(8,128)(2,1)S(1)} %concatenate.76), channel_id=1, source_target_pairs={{0,4},{4,0},{8,12},{12,8},{16,20},{20,16},{24,28},{28,24},{1,5},{5... | collective-permute-start | bytes 1153448 | tf_op jit(solution)/shard_map/ppermute | solution.py:222
  41.9 90.8 %collective-permute-start.14 = (bf16[120,3520]{1,0:T(8,128)(2,1)S(1)}, bf16[120,3520]{1,0:T(8,128)(2,1)S(1)}, u32[]{:S(2)}, u32[]{:S(2)}) collective-permute-start(bf16[120,3520]{1,0:T(8,128)(2,1)S(1)} %pad_maximum_fusion.9), channel_id=1, source_target_pairs={{0,8},{4,12},{8,0},{12,4},{16,24},{20,28},{24,16},{28,20},{1,9},{5... | collective-permute-start | bytes 2534408 | tf_op jit(solution)/shard_map/ppermute | solution.py:222
  42.3 90.9 %collective-permute-start.15 = (bf16[120,3520]{1,0:T(8,128)(2,1)S(1)}, bf16[120,3520]{1,0:T(8,128)(2,1)S(1)}, u32[]{:S(2)}, u32[]{:S(2)}) collective-permute-start(bf16[120,3520]{1,0:T(8,128)(2,1)S(1)} %pad_maximum_fusion.9), channel_id=1, source_target_pairs={{0,16},{4,20},{8,24},{12,28},{16,0},{20,4},{24,8},{28,12},{1,17},{... | collective-permute-start | bytes 2534408 | tf_op jit(solution)/shard_map/ppermute | solution.py:222
  54.1 35.8 %collective-permute-start.9 = (bf16[2,320,384]{2,1,0:T(8,128)(2,1)S(1)}, bf16[2,320,384]{2,1,0:T(8,128)(2,1)S(1)}, u32[]{:S(2)}, u32[]{:S(2)}) collective-permute-start(bf16[2,320,384]{2,1,0:T(8,128)(2,1)S(1)} %get-tuple-element.111), channel_id=1, source_target_pairs={{0,2},{1,3},{4,6},{5,7},{8,10},{9,11},{12,14},{13,15},{16,18},{17,... | collective-permute-start | bytes 1474568 | tf_op jit(solution)/shard_map/ppermute | solution.py:354
  58.6 35.5 %collective-permute-start.10 = (bf16[2,320,384]{2,1,0:T(8,128)(2,1)S(1)}, bf16[2,320,384]{2,1,0:T(8,128)(2,1)S(1)}, u32[]{:S(2)}, u32[]{:S(2)}) collective-permute-start(bf16[2,320,384]{2,1,0:T(8,128)(2,1)S(1)} %get-tuple-element.111), channel_id=1, source_target_pairs={{0,3},{4,7},{8,11},{12,15},{16,19},{20,23},{24,27},{28,31}} | collective-permute-start | bytes 1474568 | tf_op jit(solution)/shard_map/ppermute | solution.py:354
  65.7 63.1 %collective-permute-start.11 = (bf16[2,320,384]{2,1,0:T(8,128)(2,1)S(1)}, bf16[2,320,384]{2,1,0:T(8,128)(2,1)S(1)}, u32[]{:S(2)}, u32[]{:S(2)}) collective-permute-start(bf16[2,320,384]{2,1,0:T(8,128)(2,1)S(1)} %get-tuple-element.110), channel_id=1, source_target_pairs={{0,1},{1,2},{2,3},{4,5},{5,6},{6,7},{8,9},{9,10},{10,11},{12,13},{... | collective-permute-start | bytes 1474568 | tf_op jit(solution)/shard_map/ppermute | solution.py:354
  89.9 40.5 %collective-permute-start.12 = (bf16[2,320,384]{2,1,0:T(8,128)(2,1)S(1)}, bf16[2,320,384]{2,1,0:T(8,128)(2,1)S(1)}, u32[]{:S(2)}, u32[]{:S(2)}) collective-permute-start(bf16[2,320,384]{2,1,0:T(8,128)(2,1)S(1)} %get-tuple-element.110), channel_id=1, source_target_pairs={{0,2},{1,3},{4,6},{5,7},{8,10},{9,11},{12,14},{13,15},{16,18},{17,... | collective-permute-start | bytes 1474568 | tf_op jit(solution)/shard_map/ppermute | solution.py:354
  94.2 36.8 %collective-permute-start.13 = (bf16[2,320,384]{2,1,0:T(8,128)(2,1)S(1)}, bf16[2,320,384]{2,1,0:T(8,128)(2,1)S(1)}, u32[]{:S(2)}, u32[]{:S(2)}) collective-permute-start(bf16[2,320,384]{2,1,0:T(8,128)(2,1)S(1)} %get-tuple-element.110), channel_id=1, source_target_pairs={{0,3},{4,7},{8,11},{12,15},{16,19},{20,23},{24,27},{28,31}} | collective-permute-start | bytes 1474568 | tf_op jit(solution)/shard_map/ppermute | solution.py:354
  131.0 52.4 %collective-permute-start.26 = (bf16[120,5120]{1,0:T(8,128)(2,1)S(1)}, bf16[120,5120]{1,0:T(8,128)(2,1)S(1)}, u32[]{:S(2)}, u32[]{:S(2)}) collective-permute-start(bf16[120,5120]{1,0:T(8,128)(2,1)S(1)} %pad_maximum_fusion.4), channel_id=1, source_target_pairs={{0,4},{4,0},{8,12},{12,8},{16,20},{20,16},{24,28},{28,24},{1,5},{5... | collective-permute-start | bytes 3686408 | tf_op jit(solution)/shard_map/ppermute | solution.py:222
  132.7 32.7 %collective-permute-start.20 = (bf16[120,3520]{1,0:T(8,128)(2,1)S(1)}, bf16[120,3520]{1,0:T(8,128)(2,1)S(1)}, u32[]{:S(2)}, u32[]{:S(2)}) collective-permute-start(bf16[120,3520]{1,0:T(8,128)(2,1)S(1)} %pad_maximum_fusion.9), channel_id=1, source_target_pairs={{0,4},{4,0},{8,12},{12,8},{16,20},{20,16},{24,28},{28,24},{1,5},{5... | collective-permute-start | bytes 2534408 | tf_op jit(solution)/shard_map/ppermute | solution.py:222
  133.2 29.5 %collective-permute-start.18 = (bf16[56,3520]{1,0:T(8,128)(2,1)S(1)}, bf16[56,3520]{1,0:T(8,128)(2,1)S(1)}, u32[]{:S(2)}, u32[]{:S(2)}) collective-permute-start(bf16[56,3520]{1,0:T(8,128)(2,1)S(1)} %slice.529), channel_id=1, source_target_pairs={{0,16},{4,20},{8,24},{12,28},{16,0},{20,4},{24,8},{28,12},{1,17},{... | collective-permute-start | bytes 1182728 | tf_op jit(solution)/shard_map/ppermute | solution.py:222
  166.1 22.1 %collective-permute-start.27 = (bf16[120,5120]{1,0:T(8,128)(2,1)S(1)}, bf16[120,5120]{1,0:T(8,128)(2,1)S(1)}, u32[]{:S(2)}, u32[]{:S(2)}) collective-permute-start(bf16[120,5120]{1,0:T(8,128)(2,1)S(1)} %collective-permute-done.16.refs_5_), channel_id=1, source_target_pairs={{0,4},{4,0},{8,12},{12,8},{16,20},{20,16},{24,28},{28,24},{1,5},{5... | collective-permute-start | bytes 3686408 | tf_op jit(solution)/shard_map/ppermute | solution.py:222
  166.2 25.3 %collective-permute-start.28 = (bf16[120,5120]{1,0:T(8,128)(2,1)S(1)}, bf16[120,5120]{1,0:T(8,128)(2,1)S(1)}, u32[]{:S(2)}, u32[]{:S(2)}) collective-permute-start(bf16[120,5120]{1,0:T(8,128)(2,1)S(1)} %collective-permute-done.17.refs_6_), channel_id=1, source_target_pairs={{0,4},{4,0},{8,12},{12,8},{16,20},{20,16},{24,28},{28,24},{1,5},{5... | collective-permute-start | bytes 3686408 | tf_op jit(solution)/shard_map/ppermute | solution.py:222
  264.6 124.8 %collective-permute-start.30 = (bf16[480,2560]{1,0:T(8,128)(2,1)}, bf16[480,2560]{1,0:T(8,128)(2,1)}, u32[]{:S(2)}, u32[]{:S(2)}) collective-permute-start(bf16[480,2560]{1,0:T(8,128)(2,1)} %convolution_convert_fusion.4), channel_id=1, source_target_pairs={{0,4},{4,0},{8,12},{12,8},{16,20},{20,16},{24,28},{28,24},{1,5},{5... | collective-permute-start | bytes 7372808 | tf_op jit(solution)/shard_map/ppermute | solution.py:222
  265.1 129.2 %collective-permute-start.32 = (bf16[480,2560]{1,0:T(8,128)(2,1)}, bf16[480,2560]{1,0:T(8,128)(2,1)}, u32[]{:S(2)}, u32[]{:S(2)}) collective-permute-start(bf16[480,2560]{1,0:T(8,128)(2,1)} %convolution_convert_fusion), channel_id=1, source_target_pairs={{0,4},{4,0},{8,12},{12,8},{16,20},{20,16},{24,28},{28,24},{1,5},{5... | collective-permute-start | bytes 7372808 | tf_op jit(solution)/shard_map/ppermute | solution.py:222
  277.1 44.5 %collective-permute-start.34 = (bf16[2,320,384]{2,1,0:T(8,128)(2,1)S(1)}, bf16[2,320,384]{2,1,0:T(8,128)(2,1)S(1)}, u32[]{:S(2)}, u32[]{:S(2)}) collective-permute-start(bf16[2,320,384]{2,1,0:T(8,128)(2,1)S(1)} %get-tuple-element.92), channel_id=1, source_target_pairs={{1,0},{2,1},{3,2},{5,4},{6,5},{7,6},{9,8},{10,9},{11,10},{13,12},{... | collective-permute-start | bytes 1474568 | tf_op jit(solution)/shard_map/ppermute | solution.py:424
  278.7 57.0 %collective-permute-start.35 = (bf16[2,320,384]{2,1,0:T(8,128)(2,1)S(1)}, bf16[2,320,384]{2,1,0:T(8,128)(2,1)S(1)}, u32[]{:S(2)}, u32[]{:S(2)}) collective-permute-start(bf16[2,320,384]{2,1,0:T(8,128)(2,1)S(1)} %get-tuple-element.94), channel_id=1, source_target_pairs={{2,0},{3,1},{6,4},{7,5},{10,8},{11,9},{14,12},{15,13},{18,16},{19,... | collective-permute-start | bytes 1474568 | tf_op jit(solution)/shard_map/ppermute | solution.py:424
  283.4 90.1 %collective-permute-start.36 = (bf16[2,320,384]{2,1,0:T(8,128)(2,1)S(1)}, bf16[2,320,384]{2,1,0:T(8,128)(2,1)S(1)}, u32[]{:S(2)}, u32[]{:S(2)}) collective-permute-start(bf16[2,320,384]{2,1,0:T(8,128)(2,1)S(1)} %get-tuple-element.93), channel_id=1, source_target_pairs={{3,0},{7,4},{11,8},{15,12},{19,16},{23,20},{27,24},{31,28}} | collective-permute-start | bytes 1474568 | tf_op jit(solution)/shard_map/ppermute | solution.py:424
  321.6 78.3 %collective-permute-start.31 = (bf16[480,2560]{1,0:T(8,128)(2,1)S(1)}, bf16[480,2560]{1,0:T(8,128)(2,1)S(1)}, u32[]{:S(2)}, u32[]{:S(2)}) collective-permute-start(bf16[480,2560]{1,0:T(8,128)(2,1)S(1)} %convolution_convert_fusion.2), channel_id=1, source_target_pairs={{0,4},{4,0},{8,12},{12,8},{16,20},{20,16},{24,28},{28,24},{1,5},{5... | collective-permute-start | bytes 7372808 | tf_op jit(solution)/shard_map/ppermute | solution.py:222
  335.7 40.7 %collective-permute-start.47 = (bf16[2,120,384]{2,1,0:T(8,128)(2,1)S(1)}, bf16[2,120,384]{2,1,0:T(8,128)(2,1)S(1)}, u32[]{:S(2)}, u32[]{:S(2)}) collective-permute-start(bf16[2,120,384]{2,1,0:T(8,128)(2,1)S(1)} %pad_maximum_fusion.22), channel_id=1, source_target_pairs={{0,8},{4,12},{8,0},{12,4},{16,24},{20,28},{24,16},{28,20},{1,9},{5... | collective-permute-start | bytes 552968 | tf_op jit(solution)/shard_map/ppermute | solution.py:222
  404.7 86.2 %collective-permute-start.59 = (bf16[2,120,1280]{2,1,0:T(8,128)(2,1)}, bf16[2,120,1280]{2,1,0:T(8,128)(2,1)}, u32[]{:S(2)}, u32[]{:S(2)}) collective-permute-start(bf16[2,120,1280]{2,1,0:T(8,128)(2,1)} %pad_maximum_fusion.15), channel_id=1, source_target_pairs={{0,8},{4,12},{8,0},{12,4},{16,24},{20,28},{24,16},{28,20},{1,9},{5... | collective-permute-start | bytes 1843208 | tf_op jit(solution)/shard_map/ppermute | solution.py:222
  406.2 85.3 %collective-permute-start.61 = (bf16[2,120,1280]{2,1,0:T(8,128)(2,1)}, bf16[2,120,1280]{2,1,0:T(8,128)(2,1)}, u32[]{:S(2)}, u32[]{:S(2)}) collective-permute-start(bf16[2,120,1280]{2,1,0:T(8,128)(2,1)} %slice.620), channel_id=1, source_target_pairs={{0,16},{4,20},{8,24},{12,28},{16,0},{20,4},{24,8},{28,12},{1,17},{... | collective-permute-start | bytes 1843208 | tf_op jit(solution)/shard_map/ppermute | solution.py:222
  421.9 47.2 %collective-permute-start.39 = (bf16[2,320,384]{2,1,0:T(8,128)(2,1)S(1)}, bf16[2,320,384]{2,1,0:T(8,128)(2,1)S(1)}, u32[]{:S(2)}, u32[]{:S(2)}) collective-permute-start(bf16[2,320,384]{2,1,0:T(8,128)(2,1)S(1)} %get-tuple-element.96), channel_id=1, source_target_pairs={{3,0},{7,4},{11,8},{15,12},{19,16},{23,20},{27,24},{31,28}} | collective-permute-start | bytes 1474568 | tf_op jit(solution)/shard_map/ppermute | solution.py:424
  440.3 52.7 %collective-permute-start.55 = (bf16[2,120,1280]{2,1,0:T(8,128)(2,1)}, bf16[2,120,1280]{2,1,0:T(8,128)(2,1)}, u32[]{:S(2)}, u32[]{:S(2)}) collective-permute-start(bf16[2,120,1280]{2,1,0:T(8,128)(2,1)} %pad_maximum_fusion.13), channel_id=1, source_target_pairs={{0,8},{4,12},{8,0},{12,4},{16,24},{20,28},{24,16},{28,20},{1,9},{5... | collective-permute-start | bytes 1843208 | tf_op jit(solution)/shard_map/ppermute | solution.py:222
  440.8 53.7 %collective-permute-start.57 = (bf16[2,120,1280]{2,1,0:T(8,128)(2,1)}, bf16[2,120,1280]{2,1,0:T(8,128)(2,1)}, u32[]{:S(2)}, u32[]{:S(2)}) collective-permute-start(bf16[2,120,1280]{2,1,0:T(8,128)(2,1)} %slice.609), channel_id=1, source_target_pairs={{0,16},{4,20},{8,24},{12,28},{16,0},{20,4},{24,8},{28,12},{1,17},{... | collective-permute-start | bytes 1843208 | tf_op jit(solution)/shard_map/ppermute | solution.py:222
  469.0 28.3 %collective-permute-start.51 = (bf16[2,120,1280]{2,1,0:T(8,128)(2,1)}, bf16[2,120,1280]{2,1,0:T(8,128)(2,1)}, u32[]{:S(2)}, u32[]{:S(2)}) collective-permute-start(bf16[2,120,1280]{2,1,0:T(8,128)(2,1)} %pad_maximum_fusion.11), channel_id=1, source_target_pairs={{0,8},{4,12},{8,0},{12,4},{16,24},{20,28},{24,16},{28,20},{1,9},{5... | collective-permute-start | bytes 1843208 | tf_op jit(solution)/shard_map/ppermute | solution.py:222
  491.5 38.0 %collective-permute-start.40 = (bf16[480,1602]{1,0:T(8,128)(2,1)}, bf16[480,1602]{1,0:T(8,128)(2,1)S(1)}, u32[]{:S(2)}, u32[]{:S(2)}) collective-permute-start(bf16[480,1602]{1,0:T(8,128)(2,1)} %concatenate.93), channel_id=1, source_target_pairs={{0,4},{4,0},{8,12},{12,8},{16,20},{20,16},{24,28},{28,24},{1,5},{5... | collective-permute-start | bytes 4613768 | tf_op jit(solution)/shard_map/ppermute | solution.py:222
  493.0 34.2 %collective-permute-start.60 = (bf16[120,1280]{1,0:T(8,128)(2,1)S(1)}, bf16[120,1280]{1,0:T(8,128)(2,1)S(1)}, u32[]{:S(2)}, u32[]{:S(2)}) collective-permute-start(bf16[120,1280]{1,0:T(8,128)(2,1)S(1)} %get-tuple-element.76), channel_id=1, source_target_pairs={{0,16},{4,20},{8,24},{12,28},{16,0},{20,4},{24,8},{28,12},{1,17},{... | collective-permute-start | bytes 921608 | tf_op jit(solution)/shard_map/ppermute | solution.py:222
  494.5 32.8 %collective-permute-start.62 = (bf16[120,1280]{1,0:T(8,128)(2,1)S(1)}, bf16[120,1280]{1,0:T(8,128)(2,1)S(1)}, u32[]{:S(2)}, u32[]{:S(2)}) collective-permute-start(bf16[120,1280]{1,0:T(8,128)(2,1)S(1)} %get-tuple-element.77), channel_id=1, source_target_pairs={{0,8},{4,12},{8,0},{12,4},{16,24},{20,28},{24,16},{28,20},{1,9},{5... | collective-permute-start | bytes 921608 | tf_op jit(solution)/shard_map/ppermute | solution.py:222
  562.9 25.3 %collective-permute-start.45 = (bf16[120,1602]{0,1:T(8,128)(2,1)}, bf16[120,1602]{0,1:T(8,128)(2,1)}, u32[]{:S(2)}, u32[]{:S(2)}) collective-permute-start(bf16[120,1602]{0,1:T(8,128)(2,1)} %pad_maximum_fusion.19), channel_id=1, source_target_pairs={{0,1},{1,0},{2,3},{3,2},{4,5},{5,4},{6,7},{7,6},{8,9},{9,8},{10,11... | collective-permute-start | bytes 1153448 | tf_op jit(solution)/shard_map/ppermute | solution.py:262
  590.1 58.7 %collective-permute-start.46 = (bf16[120,1602]{0,1:T(8,128)(2,1)}, bf16[120,1602]{0,1:T(8,128)(2,1)S(1)}, u32[]{:S(2)}, u32[]{:S(2)}) collective-permute-start(bf16[120,1602]{0,1:T(8,128)(2,1)} %add_convert_fusion.9), channel_id=1, source_target_pairs={{0,2},{1,3},{2,0},{3,1},{4,6},{5,7},{6,4},{7,5},{8,10},{9,11},{10,... | collective-permute-start | bytes 1153448 | tf_op jit(solution)/shard_map/ppermute | solution.py:262
  (97 other events, 1119.3 us)
Sparse Core Ops, SparseCore 0:
  540.1 102.0 all-reduce.2
